TPU v7x, 32 devices: a whole 2x2x4 slice. The times are simulated.
32 devices in a mesh: wide: 8 (over z, x), narrow: 4 (over y, core).
Axes of the slice: x: 2, y: 2, z: 4, core: 2. Of those that a mesh axis runs over, the one named last changes fastest.
Arguments:
- inputs: bfloat16 [32, 256, 512], P(('wide', 'narrow')), may hold values from -6 to 6
- dense_inputs: bfloat16 [32, 256, 1536], P(('wide', 'narrow')), may hold values from -6 to 6
- lengths: int32 [32], P(('wide', 'narrow')), may hold values from 1 to 256, as said below
- owners: int32 [89], replicated, may hold values from 0 to 7, as said below
- cotangent: bfloat16 [32, 256, 512], P(('wide', 'narrow')), may hold values from -6 to 6
- master: float32 [49152, 512], P(('wide', 'narrow')), may hold values from -0.0625 to 0.0625
- moment_one: float32 [49152, 512], P(('wide', 'narrow')), may hold values from -24 to 24
- moment_two: float32 [49152, 512], P(('wide', 'narrow')), may hold values from 0.65536 to 10.6496
- average: float32 [49152, 512], P(('wide', 'narrow')), may hold values from -0.0625 to 0.0625
- norm_gain: float32 [11, 512], replicated, may hold values from 0.1 to 1.9
- norm_shift: float32 [11, 512], replicated, may hold values from -3 to 3
- norm_one: float32 [2, 11, 512], replicated, may hold values from -24 to 24
- norm_two: float32 [2, 11, 512], replicated, may hold values from 0.65536 to 10.6496
Outputs:
- block_out: bfloat16 [32, 256, 512], P(('wide', 'narrow'))
- input_grad: float32 [32, 256, 512], P(('wide', 'narrow'))
- dense_grad: float32 [32, 256, 1536], P(('wide', 'narrow'))
- weight_grad: float32 [49152, 512], P(('wide', 'narrow'))
- weight_one: float32 [49152, 512], P(('wide', 'narrow'))
- weight_two: float32 [49152, 512], P(('wide', 'narrow'))
- weight_new: float32 [49152, 512], P(('wide', 'narrow'))
- weight_average: float32 [49152, 512], P(('wide', 'narrow'))
- weight_copy: bfloat16 [49152, 512], P(('wide', 'narrow'))
- norm_grad: float32 [2, 11, 512], replicated
- norm_one_new: float32 [2, 11, 512], replicated
- norm_two_new: float32 [2, 11, 512], replicated
- norm_new: float32 [2, 11, 512], replicated
Inputs may be any that keep to these rules, and one draw needn't show every extreme that they name: `lengths`: the last utterance has exactly 256 true frames. `owners`: no owner names more than 12 matrices, and one owner names exactly 12.
All inputs are finite; a program needn't handle non-finite values.
Results may differ from a plain program's by a relative error of at most 0.014.
Values may be sent and summed in bfloat16 or wider, within the bound.
A program may use at most 512 MiB of HBM per device.

v0:
```python
import functools

import jax
import jax.numpy as jnp
from jax import lax
from jax.experimental import pallas as pl
from jax.experimental.pallas import tpu as pltpu
from jax.sharding import PartitionSpec as P

WLOW = 256
WMID = 384
K = 17
SUBS = 5
SOURCES = 6
STEP = 10
MARGIN = K // 2
EDGE = 16
UNIT = 64
F32 = jnp.float32
BF16 = jnp.bfloat16
MESH = pl.DeviceIdType.MESH
AXES = ("wide", "narrow")

norm_eps = 1e-05
beta_one = 0.9
beta_two = 0.999
adam_eps = 1e-08
rate_main = 0.02
rate_norm = 0.15
decay_main = 0.01
ema_keep = 0.8

NT = (((1,), (1,)), ((), ()))


def slot_table(owners, capacity):
    number = owners.shape[0]
    same_owner = owners[:, None] == owners[None, :]
    earlier = jnp.arange(number)[None, :] < jnp.arange(number)[:, None]
    ranking = jnp.sum(jnp.where(same_owner & earlier, 1, 0), axis=1)
    return (owners * capacity + ranking).astype(jnp.int32)


def source_pieces(half):
    pieces = []
    start = 0
    for width in (WLOW, WLOW, WLOW, WMID, WMID):
        parts = []
        stop = start + width
        while start < stop:
            chunk, lane = divmod(start, half)
            lanes = min(half - lane, stop - start)
            parts.append((chunk, lane, lanes))
            start += lanes
        pieces.append(parts)
    return pieces


class Place:
    def __init__(self, depth):
        wide = lax.axis_index("wide")
        narrow = lax.axis_index("narrow")
        self.depth = depth
        self.core = lax.rem(narrow, 2)
        self.y = narrow // 2
        self.x = lax.rem(wide, 2)
        self.z = wide // 2
        self.groups = depth * 4
        self.me = wide * 2 + self.y

    def at(self, z, x, y, core):
        return (z * 2 + x, y * 2 + core)

    def beside(self):
        return self.at(self.z + 1 - 2 * lax.rem(self.z, 2), self.x, self.y, self.core)

    def partner(self):
        return self.at(self.z, self.x, self.y, 1 - self.core)

    def over_x(self):
        return self.at(self.z, 1 - self.x, self.y, self.core)

    def over_y(self):
        return self.at(self.z, self.x, 1 - self.y, self.core)

    def up(self):
        return self.at(self.z + 1, self.x, self.y, self.core)

    def down(self):
        return self.at(self.z - 1, self.x, self.y, self.core)

    def peer(self, offset):
        other = lax.rem(self.me + offset, self.groups)
        return (other // 2, lax.rem(other, 2) * 2 + self.core)

    def enter(self):
        barrier = pltpu.get_barrier_semaphore()
        pl.semaphore_signal(barrier, inc=1, device_id=self.partner(), device_id_type=MESH)

        def greet(offset, carry):
            pl.semaphore_signal(barrier, inc=1, device_id=self.peer(offset), device_id_type=MESH)
            return carry

        lax.fori_loop(1, self.groups, greet, 0)
        pl.semaphore_wait(barrier, self.groups)


class QuadPlace(Place):
    def __init__(self, depth):
        super().__init__(depth)
        self.parity = lax.rem(self.z, 2)
        self.z = self.z // 2

    def at(self, z, x, y, core):
        return ((2 * z + self.parity) * 2 + x, y * 2 + core)

    def enter(self):
        barrier = pltpu.get_barrier_semaphore()

        def greet(device):
            pl.semaphore_signal(barrier, inc=1, device_id=device, device_id_type=MESH)

        for device in (self.partner(), self.over_x(), self.over_y()):
            greet(device)
        above, below = self.z + 1 < self.depth, self.z >= 1
        pl.when(above)(functools.partial(greet, self.up()))
        pl.when(below)(functools.partial(greet, self.down()))
        met = 3 + above.astype(jnp.int32) + below.astype(jnp.int32)
        pl.semaphore_wait(barrier, met)


def remote(src, dst, send_sem, recv_sem, device):
    return pltpu.make_async_remote_copy(
        src_ref=src,
        dst_ref=dst,
        send_sem=send_sem,
        recv_sem=recv_sem,
        device_id=device,
        device_id_type=MESH,
    )


def when(cond, action):
    if cond is None:
        action()
    else:
        pl.when(cond)(action)


def cut(block, share):
    units = block // UNIT
    small = max(1, units // share)
    return (units - 2 * small) // 2 * UNIT, small * UNIT


def steps(depth, body, first=0):
    if depth <= 4:
        for step in range(first, depth):
            body(step)
    else:
        def looped(step, carry):
            body(step)
            return carry

        if first == 0:
            body(0)
        lax.fori_loop(max(first, 1), depth, looped, 0)


def tree_sems(depth):
    dma = pltpu.SemaphoreType.DMA
    return [
        dma((depth, 2)), dma((depth,)), dma((depth, 2, 4)), dma((depth, 4)),
        dma((depth,)), dma((depth,)), dma((depth, 2)), dma((depth, 2)),
        dma((depth,)), dma((depth,)), dma((depth, 2)), dma((depth, 2)),
        dma((6,)), dma((6,)),
    ]


def gather_bank(place, bank, block, sems, meanwhile=lambda: None):
    depth, z, x, y = place.depth, place.z, place.x, place.y
    large, small = cut(block, 9)
    (zab_s, zab_r, zcd_s, zcd_r, ax_s, ax_r, ay_s, ay_r, by_s, by_r, bx_s, bx_r, cd_s, cd_r) = sems

    def rows(zz, xx, yy, first, count):
        begin = ((zz * 2 + xx) * 2 + yy) * (block // UNIT) + first // UNIT
        return bank.at[pl.ds(begin, count // UNIT)]

    def move(zz, xx, yy, first, count, send_sem, recv_sem, device):
        ref = rows(zz, xx, yy, first, count)
        return remote(ref, ref, send_sem, recv_sem, device)

    start_b, start_c, start_d = large, 2 * large, 2 * large + small
    over_x, over_y, up, down = place.over_x(), place.over_y(), place.up(), place.down()

    def sides(step):
        out = [(z - step, z - step >= 0)]
        if not (isinstance(step, int) and step == 0):
            out.append((z + step, z + step < depth))
        return out

    def z_moves(step, kind):
        out = []
        low, high = z - step, z + step
        for level, cond, device, way in (
            (low, (low >= 0) & (z + 1 < depth), up, 0),
            (high, (high < depth) & (z >= 1), down, 1),
        ):
            if kind == "ab":
                out.append(
                    (cond, move(level, x, y, 0, 2 * large, zab_s.at[level, way], zab_r.at[level], device))
                )
            else:
                for xx in range(2):
                    for yy in range(2):
                        out.append(
                            (
                                cond,
                                move(
                                    level, xx, yy, start_c, 2 * small,
                                    zcd_s.at[level, way, xx * 2 + yy],
                                    zcd_r.at[level, xx * 2 + yy], device,
                                ),
                            )
                        )
        return out

    def ax(level):
        return move(level, x, y, 0, large, ax_s.at[level], ax_r.at[level], over_x)

    def by(level):
        return move(level, x, y, start_b, large, by_s.at[level], by_r.at[level], over_y)

    def ay(level, other):
        xx = 1 - x if other else x
        return move(level, xx, y, 0, large, ay_s.at[level, other], ay_r.at[level, other], over_y)

    def bx(level, other):
        yy = 1 - y if other else y
        return move(level, x, yy, start_b, large, bx_s.at[level, other], bx_r.at[level, other], over_x)

    plane = [
        move(z, x, y, start_c, small, cd_s.at[0], cd_r.at[0], over_x),
        move(z, x, y, start_d, small, cd_s.at[1], cd_r.at[1], over_y),
        move(z, x, y, start_c, small, cd_s.at[2], cd_r.at[2], over_y),
        move(z, 1 - x, y, start_c, small, cd_s.at[3], cd_r.at[3], over_y),
        move(z, x, y, start_d, small, cd_s.at[4], cd_r.at[4], over_x),
        move(z, x, 1 - y, start_d, small, cd_s.at[5], cd_r.at[5], over_x),
    ]

    def run(step):
        if isinstance(step, int) and step == 0:
            plane[0].start()
            plane[1].start()
        else:
            for level, cond in sides(step):
                when(cond, move(level, x, y, 0, 2 * large, zab_s.at[level, 0], zab_r.at[level], up).wait_recv)
        for cond, copy in z_moves(step, "ab"):
            when(cond, copy.start)
        for level, cond in sides(step):
            def begin(level=level):
                ax(level).start()
                by(level).start()
                ay(level, 0).start()
                bx(level, 0).start()

            when(cond, begin)
        if isinstance(step, int) and step == 0:
            meanwhile()
            plane[2].start()
            plane[4].start()
            plane[0].wait_recv()
            plane[3].start()
            plane[1].wait_recv()
            plane[5].start()
            for copy in plane[2:]:
                copy.wait_recv()
            for cond, copy in z_moves(0, "cd"):
                when(cond, copy.start)
        for level, cond in sides(step):
            def across(level=level):
                ax(level).wait_recv()
                ay(level, 1).start()
                by(level).wait_recv()
                bx(level, 1).start()

            when(cond, across)
        if not (isinstance(step, int) and step == 0):
            for level, cond in sides(step):
                def arrived(level=level):
                    for part in range(4):
                        move(
                            level, x, y, start_c, 2 * small, zcd_s.at[level, 0, part],
                            zcd_r.at[level, part], up,
                        ).wait_recv()

                when(cond, arrived)
            for cond, copy in z_moves(step, "cd"):
                when(cond, copy.start)

    steps(depth, run)

    def drain(step):
        for level, cond in sides(step):
            def finish(level=level):
                for other in range(2):
                    ay(level, other).wait_recv()
                    bx(level, other).wait_recv()
                    ay(level, other).wait_send()
                    bx(level, other).wait_send()
                ax(level).wait_send()
                by(level).wait_send()

            when(cond, finish)
        for kind in ("ab", "cd"):
            for cond, copy in z_moves(step, kind):
                when(cond, copy.wait_send)

    steps(depth, drain)
    for copy in plane:
        copy.wait_send()


def strips(rows, body, carry=0):
    strip = 64

    def one(index, carry):
        return body(pl.ds(pl.multiple_of(index * strip, strip), strip), carry)

    return lax.fori_loop(0, rows // strip, one, carry)


def fold(values):
    return jnp.sum(values.reshape(-1, 8, values.shape[1]), axis=0)


def chain_kernel(
    depth, block,
    slot_ref, length_ref, master, own_x, own_dense, own_cot, gain_ref, shift_ref,
    act_out, dcv_out, res_out, blk_out, ig_out, dg_out, nrm_out,
    bank, act, dense, mask, cot, raw, side, pre4, slope, upown, upsend, uprecv, dcv, dsd, res, dgrecv,
    igrecv, stage, nrm, blk, blksend, keep, ex_side, ex_last, ex_sub,
    load_sem, swap_s, swap_r, act_s, act_r, up_s, up_r, ex_s, ex_r, out_sem, far_s, far_r, near_s, near_r,
    *tree,
):
    place = Place(depth)
    core, other = place.core, 1 - place.core
    partner, beside = place.partner(), place.beside()
    half = bank.shape[2]
    width = 2 * half
    frames = mask.shape[1]
    rows = 2 * frames
    peers = place.groups - 1
    chunks = dense.shape[0]
    pieces = source_pieces(half)
    inner = pl.ds(EDGE, frames)
    own_rows = block // 2
    load_rows = min(own_rows, rows)
    loads_of = own_rows // load_rows

    mats_in = []
    for part in range(loads_of):
        for h in range(2):
            mats_in.append(
                pltpu.make_async_copy(
                    master.at[pl.ds(part * load_rows, load_rows), pl.ds(h * half, half)],
                    side.at[part * 2 + h, pl.ds(0, load_rows)],
                    load_sem.at[part * 2 + h],
                )
            )
    x_in = [
        pltpu.make_async_copy(
            own_x.at[0, :, pl.ds(h * half, half)], act.at[0, h, core, inner], load_sem.at[6 + h]
        )
        for h in range(2)
    ]
    dense_in = [
        pltpu.make_async_copy(
            own_dense.at[0, :, pl.ds(chunk * half, half)], dense.at[chunk, core], load_sem.at[8 + chunk]
        )
        for chunk in range(chunks)
    ]
    ours_lanes = pl.ds(pl.multiple_of(core * half, half), half)
    theirs_lanes = pl.ds(pl.multiple_of(other * half, half), half)
    cot_in = pltpu.make_async_copy(own_cot.at[0, :, ours_lanes], cot.at[core], load_sem.at[8 + chunks])
    for copy in mats_in + x_in + dense_in + [cot_in]:
        copy.start()
    place.enter()
    base = place.me * (block // UNIT) + core * (own_rows // UNIT)
    units = load_rows // UNIT
    for copy in mats_in:
        copy.wait()
    for part in range(loads_of):
        def narrow(unit, carry, part=part):
            at = pl.ds(pl.multiple_of(unit * UNIT, UNIT), UNIT)
            stage[part * units + unit] = side[part * 2 + other, at].astype(BF16)
            bank[base + part * units + unit] = side[part * 2 + core, at].astype(BF16)
            return carry

        lax.fori_loop(0, units, narrow, 0)
    send_mats = remote(stage, bank.at[pl.ds(base, own_rows // UNIT)], swap_s.at[0], swap_r.at[0], partner)
    send_mats.start()
    mask[core] = (
        lax.broadcasted_iota(jnp.int32, (frames, 128), 0) < length_ref[0]
    ).astype(F32)
    edge_zero = jnp.zeros((EDGE, half), BF16)

    def clear(section, carry):
        for u in range(2):
            for h in range(2):
                act[section, h, u, pl.ds(0, EDGE)] = edge_zero
                act[section, h, u, pl.ds(EDGE + frames, EDGE)] = edge_zero
            dcv[section, u, pl.ds(0, EDGE)] = edge_zero
            dcv[section, u, pl.ds(EDGE + frames, EDGE)] = edge_zero
        return carry

    lax.fori_loop(0, SUBS, clear, 0)
    send_mats.wait()

    def prepare():
        for copy in x_in + dense_in + [cot_in]:
            copy.wait()
        low_mask = jnp.concatenate([mask[core].astype(BF16)] * (half // 128), axis=1)
        for h in range(2):
            act[0, h, core, inner] = act[0, h, core, inner] * low_mask
        for chunk in range(chunks):
            dense[chunk, core] = dense[chunk, core] * low_mask
        own = act.at[0, :, core, inner]
        swaps = [
            remote(own, own, swap_s.at[1], swap_r.at[1], partner),
            remote(dense.at[:, core], dense.at[:, core], swap_s.at[2], swap_r.at[2], partner),
            remote(mask.at[core], mask.at[core], swap_s.at[3], swap_r.at[3], partner),
            remote(own_cot.at[0, :, theirs_lanes], cot.at[core], swap_s.at[4], swap_r.at[4], partner),
        ]
        for copy in swaps:
            copy.start()
        return swaps

    swaps = []
    gather_bank(place, bank, block, tree, lambda: swaps.extend(prepare()))
    for copy in swaps:
        copy.wait()

    outs = []

    def put(src, dst):
        copy = pltpu.make_async_copy(src, dst, out_sem.at[len(outs)])
        copy.start()
        outs.append(copy)

    def far_act(section):
        return remote(
            act.at[section, core, :, inner], act_out.at[section, 1, core],
            far_s.at[section], far_r.at[section], beside,
        )

    def near_act(section):
        ref = act_out.at[section, 1, core]
        return remote(ref, ref, near_s.at[section], near_r.at[section], partner)

    def far_dcv(section):
        return remote(
            dcv.at[section], dcv_out.at[section, 1],
            far_s.at[SUBS + section], far_r.at[SUBS + section], beside,
        )

    def far_res(index):
        return remote(
            res.at[index], res_out.at[1, index],
            far_s.at[2 * SUBS + index], far_r.at[2 * SUBS + index], beside,
        )

    far_act(0).start()

    def weight(matrix, first, count):
        begin = slot_ref[matrix] * (width // UNIT) + first // UNIT
        return jnp.concatenate([bank[begin + i] for i in range(count // UNIT)], axis=0)

    def valid(at):
        return jnp.concatenate([mask_rows(at)] * (half // 128), axis=1)

    def mask_rows(at):
        return mask[at.start // frames, pl.ds(pl.multiple_of(lax.rem(at.start, frames), 64), at.size)]

    def gain(index):
        return gain_ref[pl.ds(index, 1), ours_lanes]

    def bias(index):
        return shift_ref[pl.ds(index, 1), ours_lanes]

    def share(buffer, index, values):
        buffer[place.me] = values

        def go(offset, carry):
            remote(
                buffer.at[place.me], buffer.at[place.me], ex_s.at[index], ex_r.at[index],
                place.peer(offset),
            ).start()
            return carry

        lax.fori_loop(1, place.groups, go, 0, unroll=place.groups <= 16)

    def shared(buffer, index):
        everyone = buffer.at[pl.ds(0, peers)]
        copy = remote(everyone, everyone, ex_s.at[index], ex_r.at[index], place.peer(1))
        copy.wait_recv()
        copy.wait_send()
        return buffer[...]

    def total_of(values):
        return jnp.sum(values, axis=0, keepdims=True)

    def counted():
        def add(at, carry):
            return carry + fold(valid(at))

        return total_of(strips(rows, add, jnp.zeros((8, half), F32)))

    def moments(load, count):
        pivot = load(pl.ds(0, 8))[0:1]

        def add(at, carry):
            first, second = carry
            valid_now = valid(at)
            off = (load(at) - pivot) * valid_now
            return first + fold(off), second + fold(off * off)

        zero = jnp.zeros((8, half), F32)
        first, second = strips(rows, add, (zero, zero))
        first, second = total_of(first), total_of(second)
        return first + count * pivot, jnp.maximum(second - first * first / count, 0.0)

    def merge(count, total, squares):
        frame_total = jnp.sum(count, axis=0)
        mean = jnp.sum(total, axis=0) / frame_total
        shift = total / count - mean[None]
        variance = jnp.sum(squares + count * shift * shift, axis=0) / frame_total
        return mean[None], lax.rsqrt(variance + norm_eps)[None], frame_total[None]

    def save(index, mean, inverse):
        scale = gain(index) * inverse
        keep[0, pl.ds(index, 1)] = inverse
        keep[1, pl.ds(index, 1)] = mean * inverse
        keep[2, pl.ds(index, 1)] = scale
        keep[3, pl.ds(index, 1)] = bias(index) - mean * scale

    def kept(row, index):
        return keep[row, pl.ds(index, 1)]

    count = counted()
    totals, squares = [], []
    for index in range(SOURCES):
        value = None
        if index < SOURCES - 1:
            for chunk, lane, lanes in pieces[index]:
                left = dense[chunk].reshape(rows, half)[:, lane : lane + lanes]
                right = weight(SUBS * K + chunk // 2, (chunk % 2) * half + lane, lanes)
                term = jnp.dot(left, right, preferred_element_type=F32)
                value = term if value is None else value + term
        else:
            for h in range(2):
                left = jnp.concatenate([act[0, h, u, inner] for u in range(2)], axis=0)
                term = jnp.dot(left, weight(SUBS * K + 3, h * half, half), preferred_element_type=F32)
                value = term if value is None else value + term
        side[index] = value
        total, square = moments(lambda at, index=index: side[index, at], count)
        totals.append(total)
        squares.append(square)
    fill = jnp.zeros((3, half), F32)
    share(ex_side, 0, jnp.concatenate([count] + totals + squares + [fill], axis=0))

    def convolve(section, h, first):
        value = None
        for k in range(K):
            left = jnp.concatenate(
                [act[section, h, u, pl.ds(EDGE - MARGIN + k, frames)] for u in range(2)], axis=0
            )
            term = jnp.dot(
                left, weight(section * K + k, h * half, half), preferred_element_type=F32
            )
            value = term if value is None else value + term
            if k % 2 == 1 or k == K - 1:
                if first and k == 1:
                    raw[section] = value
                else:
                    raw[section] += value
                value = None

    def swap_act(section):
        own = act.at[section, core, :, inner]
        return remote(own, own, act_s.at[section], act_r.at[section], partner)

    def forward(section, last):
        convolve(section, core, True)
        if isinstance(section, int):
            if section > 0:
                swap_act(section).wait_recv()
        else:
            pl.when(section > 0)(swap_act(section).wait_recv)
        convolve(section, other, False)
        total, square = moments(lambda at: raw[section, at], count)
        buffer = ex_sub.at[lax.rem(section, 2)]
        share(buffer, 1 + section, jnp.concatenate([count, total, square, jnp.zeros_like(count)], axis=0))
        parts = shared(buffer, 1 + section)
        mean, inverse, frame_total = merge(parts[:, 0], parts[:, 1], parts[:, 2])
        save(section, mean, inverse)
        scale, offset = kept(2, section), kept(3, section)

        def activate(at, carry):
            before = raw[section, at] * scale + offset
            if last:
                before = before + pre4[at]
                pre4[at] = before
            hidden = (before * jax.nn.sigmoid(before) * valid(at)).astype(BF16)
            u = at.start // frames
            first = pl.multiple_of(lax.rem(at.start, frames), 64)
            if last:
                @pl.when(u == core)
                def _():
                    blk[core, pl.ds(first, at.size)] = hidden

                @pl.when(u != core)
                def _():
                    blksend[pl.ds(first, at.size)] = hidden
            else:
                act[section + 1, core, u, pl.ds(pl.multiple_of(first + EDGE, EDGE), at.size)] = hidden
            return carry

        strips(rows, activate)
        if not last:
            swap_act(section + 1).start()
            far_act(section + 1).start()
            far_act(section).wait_recv()
            near_act(section).start()
        return frame_total

    def looped(section, carry):
        forward(section, False)

        @pl.when(section == 0)
        def _():
            parts = shared(ex_side, 0)
            for index in range(SOURCES):
                mean, inverse, _ = merge(
                    parts[:, 0], parts[:, 1 + index], parts[:, 1 + SOURCES + index]
                )
                save(SUBS + index, mean, inverse)
            scales = [kept(2, SUBS + index) for index in range(SOURCES)]
            offset = sum(kept(3, SUBS + index) for index in range(SOURCES))

            def add(at, carry):
                before = offset
                for index in range(SOURCES):
                    before = before + side[index, at] * scales[index]
                pre4[at] = before
                return carry

            strips(rows, add)

        return carry

    lax.fori_loop(0, SUBS - 1, looped, 0)
    frame_total = forward(SUBS - 1, True)
    blk_copy = remote(blksend, blk.at[core], swap_s.at[5], swap_r.at[5], partner)
    blk_copy.start()
    for section in range(1, SUBS):
        swap_act(section).wait_send()
    for h in range(2):
        put(act.at[:, h, :, inner], act_out.at[:, 0, h])
    far_act(SUBS - 1).wait_recv()
    near_act(SUBS - 1).start()

    def hat_of(values, index):
        return values * kept(0, index) - kept(1, index)

    def back_half(section, h):
        total = None
        value = None
        for k in range(K):
            left = jnp.concatenate(
                [dcv[section, u, pl.ds(EDGE + MARGIN - k, frames)] for u in range(2)], axis=0
            )
            term = lax.dot_general(
                left, weight(section * K + k, h * half, half), NT, preferred_element_type=F32
            )
            value = term if value is None else value + term
            if k % 2 == 1 or k == K - 1:
                total = value if total is None else total + value
                value = None
        return total

    def up_copy(section):
        slot = lax.rem(section, 2)
        return remote(upsend, uprecv.at[slot], up_s.at[slot], up_r.at[slot], partner)

    def backward(section):
        upsend[...] = back_half(section, other)
        up_copy(section).start()
        upown[...] = back_half(section, core)

    def slopes(section, upstream, before_of, others):
        sources = [(lambda at: raw[section, at], section)] + others

        def one(at, carry):
            before = before_of(at)
            sigmoid = jax.nn.sigmoid(before)
            now = upstream(at) * valid(at) * (sigmoid * (1.0 + before * (1.0 - sigmoid)))
            slope[at] = now
            out = [carry[0] + fold(now)]
            for (load, index), so_far in zip(sources, carry[1:]):
                out.append(so_far + fold(now * hat_of(load(at), index)))
            return tuple(out)

        zero = jnp.zeros((8, half), F32)
        return [total_of(value) for value in strips(rows, one, (zero,) * (1 + len(sources)))]

    def branch(load, index, shift_sum, gain_sum, store):
        scale = kept(2, index)
        shift_mean, gain_mean = shift_sum / frame_total, gain_sum / frame_total

        def one(at, carry):
            value = slope[at] - shift_mean - hat_of(load(at), index) * gain_mean
            store(at, (valid(at) * scale * value).astype(BF16))
            return carry

        strips(rows, one)

    def conv_branch(section, shift_sum, gain_sum):
        def store(at, value):
            first = pl.multiple_of(lax.rem(at.start, frames) + EDGE, EDGE)
            dcv[section, at.start // frames, pl.ds(first, at.size)] = value

        branch(lambda at: raw[section, at], section, shift_sum, gain_sum, store)
        far_dcv(section).start()

    def cot_at(at):
        return cot[
            at.start // frames, pl.ds(pl.multiple_of(lax.rem(at.start, frames), 64), at.size)
        ].astype(F32)

    sums = slopes(
        SUBS - 1, cot_at, lambda at: pre4[at],
        [(lambda at, index=index: side[index, at], SUBS + index) for index in range(SOURCES)],
    )
    share(ex_last, SUBS + 1, jnp.concatenate(sums, axis=0))
    sums = jnp.sum(shared(ex_last, SUBS + 1), axis=0)
    shift_sum = sums[0:1]
    conv_branch(SUBS - 1, shift_sum, sums[1:2])
    nrm[core] = jnp.zeros_like(nrm[0])
    nrm[core, pl.ds(SUBS - 1, 1 + SOURCES)] = sums[1:]
    nrm[core, pl.ds(SUBS + SOURCES + SUBS - 1, 1)] = shift_sum
    backward(SUBS - 1)
    for index in range(SOURCES):
        def store(at, value, index=index):
            dsd[index, at] = value

        branch(
            lambda at, index=index: side[index, at], SUBS + index, shift_sum,
            sums[2 + index : 3 + index], store,
        )
    theirs = pl.multiple_of(other * frames, frames)
    ours = pl.multiple_of(core * frames, frames)
    dg_copy = remote(
        side.at[:, pl.ds(theirs, frames)], dgrecv, swap_s.at[6], swap_r.at[6], partner
    )

    def dense_grads():
        for index in range(SOURCES - 1):
            for chunk, lane, lanes in pieces[index]:
                right = weight(SUBS * K + chunk // 2, (chunk % 2) * half + lane, lanes)
                side[chunk, :, pl.ds(lane, lanes)] = lax.dot_general(
                    dsd[index], right, NT, preferred_element_type=F32
                )
        dg_copy.start()

    def residual_grads():
        rows_of = [[] for _ in range(chunks)]
        for index, parts in enumerate(pieces):
            for chunk, lane, lanes in parts:
                rows_of[chunk].append((lane, lanes, index))
        for chunk in range(chunks):
            turned = dense[chunk].reshape(rows, half).T
            for lane, lanes, index in rows_of[chunk]:
                res[chunk // 2, pl.ds((chunk % 2) * half + lane, lanes)] = jnp.dot(
                    turned[lane : lane + lanes], dsd[index], preferred_element_type=F32
                ).astype(BF16)
        for h in range(2):
            turned = jnp.concatenate([act[0, h, u, inner] for u in range(2)], axis=0).T
            res[3, pl.ds(h * half, half)] = jnp.dot(
                turned, dsd[SOURCES - 1], preferred_element_type=F32
            ).astype(BF16)

    def looped_back(turn, carry):
        section = SUBS - 2 - turn
        copy = up_copy(section + 1)
        copy.wait()
        slot = lax.rem(section + 1, 2)
        scale, offset = kept(2, section), kept(3, section)
        sums = slopes(
            section, lambda at: upown[at] + uprecv[slot, at],
            lambda at: raw[section, at] * scale + offset, [],
        )
        zero = jnp.zeros((2, half), F32)
        buffer = ex_sub.at[lax.rem(section, 2)]
        share(buffer, SUBS + 2 + section, jnp.concatenate(sums + [zero], axis=0))

        @pl.when(section == SUBS - 2)
        def _():
            residual_grads()
            dense_grads()

        sums = jnp.sum(shared(buffer, SUBS + 2 + section), axis=0)
        far_res(turn).start()
        conv_branch(section, sums[0:1], sums[1:2])
        nrm[core, pl.ds(section, 1)] = sums[1:2]
        nrm[core, pl.ds(SUBS + SOURCES + section, 1)] = sums[0:1]

        @pl.when(section > 0)
        def _():
            backward(section)

        return carry

    lax.fori_loop(0, SUBS - 1, looped_back, 0)
    put(dcv, dcv_out.at[:, 0])
    put(res, res_out.at[0])
    nrm_copy = remote(nrm.at[core], nrm.at[core], swap_s.at[7], swap_r.at[7], partner)
    nrm_copy.start()
    for h in range(2):
        uprecv[h] = back_half(0, h) + lax.dot_general(
            dsd[SOURCES - 1], weight(SUBS * K + 3, h * half, half), NT, preferred_element_type=F32
        )
    ig_copy = remote(
        uprecv.at[:, pl.ds(theirs, frames)], igrecv, swap_s.at[8], swap_r.at[8], partner
    )
    ig_copy.start()
    own_valid = jnp.concatenate([mask[core]] * (half // 128), axis=1)
    dg_copy.wait()
    for chunk in range(chunks):
        dgrecv[chunk] = (dgrecv[chunk] + side[chunk, pl.ds(ours, frames)]) * own_valid
        put(dgrecv.at[chunk], dg_out.at[0, :, pl.ds(chunk * half, half)])
    blk_copy.wait()
    nrm_copy.wait()
    put(nrm, nrm_out)
    ig_copy.wait()
    for h in range(2):
        igrecv[h] = (igrecv[h] + uprecv[h, pl.ds(ours, frames)]) * own_valid
        put(igrecv.at[h], ig_out.at[0, :, pl.ds(h * half, half)])
        put(blk.at[h], blk_out.at[0, :, pl.ds(h * half, half)])
    for section in range(SUBS):
        near_act(section).wait()
        far_act(section).wait_send()
        far_dcv(section).wait()
    for index in range(4):
        far_res(index).wait()
    for copy in outs:
        copy.wait()


def run_chain(depth, block, places, lengths, master, x, dense, cot, gains, shifts):
    frames, width = x.shape[1:]
    half = width // 2
    rows = 2 * frames
    chunks = dense.shape[2] // half
    padded = frames + 2 * EDGE
    groups = depth * 4
    dma = pltpu.SemaphoreType.DMA
    anywhere = pl.BlockSpec(memory_space=pl.ANY)
    vmem = pl.BlockSpec(memory_space=pltpu.VMEM)
    smem = pl.BlockSpec(memory_space=pltpu.SMEM)
    out_shape = [
        jax.ShapeDtypeStruct((SUBS, 2, 2, 2, frames, half), BF16),
        jax.ShapeDtypeStruct((SUBS, 2, 2, padded, half), BF16),
        jax.ShapeDtypeStruct((2, 4, width, half), BF16),
        jax.ShapeDtypeStruct(x.shape, BF16),
        jax.ShapeDtypeStruct(x.shape, F32),
        jax.ShapeDtypeStruct(dense.shape, F32),
        jax.ShapeDtypeStruct((2, 16, half), F32),
    ]
    scratch = [
        pltpu.VMEM((groups * block // UNIT, UNIT, half), BF16),
        pltpu.VMEM((SUBS, 2, 2, padded, half), BF16),
        pltpu.VMEM((chunks, 2, frames, half), BF16),
        pltpu.VMEM((2, frames, 128), F32),
        pltpu.VMEM((2, frames, half), BF16),
        pltpu.VMEM((SUBS, rows, half), F32),
        pltpu.VMEM((SOURCES, rows, half), F32),
        pltpu.VMEM((rows, half), F32),
        pltpu.VMEM((rows, half), F32),
        pltpu.VMEM((rows, half), F32),
        pltpu.VMEM((rows, half), F32),
        pltpu.VMEM((2, rows, half), F32),
        pltpu.VMEM((SUBS, 2, padded, half), BF16),
        pltpu.VMEM((SOURCES, rows, half), BF16),
        pltpu.VMEM((4, width, half), BF16),
        pltpu.VMEM((chunks, frames, half), F32),
        pltpu.VMEM((2, frames, half), F32),
        pltpu.VMEM((block // 2 // UNIT, UNIT, half), BF16),
        pltpu.VMEM((2, 16, half), F32),
        pltpu.VMEM((2, frames, half), BF16),
        pltpu.VMEM((frames, half), BF16),
        pltpu.VMEM((4, 16, half), F32),
        pltpu.VMEM((groups, 16, half), F32),
        pltpu.VMEM((groups, 8, half), F32),
        pltpu.VMEM((2, groups, 4, half), F32),
        dma((9 + chunks,)),
        dma((9,)), dma((9,)),
        dma((SUBS,)), dma((SUBS,)),
        dma((2,)), dma((2,)),
        dma((2 * SUBS + 1,)), dma((2 * SUBS + 1,)),
        dma((10 + chunks,)),
        dma((2 * SUBS + 4,)), dma((2 * SUBS + 4,)),
        dma((SUBS,)), dma((SUBS,)),
    ] + tree_sems(depth)
    return pl.pallas_call(
        functools.partial(chain_kernel, depth, block),
        out_shape=out_shape,
        in_specs=[smem] * 2 + [anywhere] * 4 + [vmem] * 2,
        out_specs=[anywhere] * len(out_shape),
        scratch_shapes=scratch,
        compiler_params=pltpu.CompilerParams(
            collective_id=1, has_side_effects=True, vmem_limit_bytes=63 << 20
        ),
        cost_estimate=pl.CostEstimate(
            flops=4 * SUBS * K * rows * width * half, bytes_accessed=16 << 20, transcendentals=0
        ),
        name="chain",
    )(places, lengths, master, x, dense, cot, gains, shifts)


def grad_kernel(slot_ref, act_ref, dcv_ref, res_ref, out_ref, left, stage, count, sems):
    section = pl.program_id(0)
    half = act_ref.shape[5]
    width = 2 * half
    frames = act_ref.shape[4]
    rows = 2 * frames
    ring = stage.shape[0]
    for pair in range(2):
        for h in range(2):
            left[pl.ds(h * half, half), pl.ds(pair * rows, rows)] = (
                act_ref[0, pair, h].reshape(rows, half).T
            )

    @pl.when(section == 0)
    def _():
        count[0] = 0

    def slot_copy(place, slot):
        out = out_ref.at[pl.ds(pl.multiple_of(slot * width, 16), width)]
        return pltpu.make_async_copy(stage.at[place], out, sems.at[place])

    def emit(matrix, compute):
        slot = slot_ref[matrix]

        @pl.when(slot >= 0)
        def _():
            turn = count[0]
            place = lax.rem(turn, ring)
            pl.when(turn >= ring)(slot_copy(place, 0).wait)
            stage[place] = compute().astype(BF16)
            slot_copy(place, slot).start()
            count[0] = turn + 1

    for k in range(K):
        def conv(k=k):
            right = jnp.concatenate(
                [
                    dcv_ref[0, pair, u, pl.ds(EDGE + MARGIN - k, frames)]
                    for pair in range(2)
                    for u in range(2)
                ],
                axis=0,
            )
            return jnp.dot(left[...], right, preferred_element_type=F32)

        emit(section * K + k, conv)

    @pl.when(section == SUBS - 1)
    def _():
        for index in range(4):
            emit(
                SUBS * K + index,
                lambda index=index: res_ref[0, index].astype(F32) + res_ref[1, index].astype(F32),
            )
        turns = count[0]

        def finish(place, carry):
            pl.when(place < turns)(slot_copy(place, 0).wait)
            return carry

        lax.fori_loop(0, ring, finish, 0)


def run_grads(total_rows, places, act, dcv, res):
    half = act.shape[5]
    frames = act.shape[4]
    ring = 8
    grid_spec = pltpu.PrefetchScalarGridSpec(
        num_scalar_prefetch=1,
        grid=(SUBS,),
        in_specs=[
            pl.BlockSpec((1,) + act.shape[1:], lambda s, t: (s, 0, 0, 0, 0, 0)),
            pl.BlockSpec((1,) + dcv.shape[1:], lambda s, t: (s, 0, 0, 0, 0)),
            pl.BlockSpec(res.shape, lambda s, t: (0, 0, 0, 0)),
        ],
        out_specs=pl.BlockSpec(memory_space=pl.ANY),
        scratch_shapes=[
            pltpu.VMEM((2 * half, 4 * frames), BF16),
            pltpu.VMEM((ring, 2 * half, half), BF16),
            pltpu.SMEM((1,), jnp.int32),
            pltpu.SemaphoreType.DMA((ring,)),
        ],
    )
    return pl.pallas_call(
        grad_kernel,
        grid_spec=grid_spec,
        out_shape=jax.ShapeDtypeStruct((total_rows, half), BF16),
        compiler_params=pltpu.CompilerParams(vmem_limit_bytes=60 << 20),
        name="weight_grads",
    )(places, act, dcv, res)


def reduce_kernel(
    depth, block, grads, out, l_ay, l_ax, l_bx, l_by, l_zab, l_zcd, l_c, l_d, stage, final, result,
    stage_sem, out_sem, swap_s, swap_r, ay_s, ay_r, ax_s, ax_r, bx_s, bx_r, by_s, by_r,
    zab_s, zab_r, zcd_s, zcd_r, cd_s, cd_r,
):
    place = QuadPlace(depth)
    z, x, y, core = place.z, place.x, place.y, place.core
    large, small = cut(block, 16)
    start_b, start_c, start_d = large, 2 * large, 2 * large + small
    over_x, over_y, up, down = place.over_x(), place.over_y(), place.up(), place.down()
    place.enter()

    def rows(zz, xx, yy, first, count):
        begin = pl.multiple_of(((zz * 2 + xx) * 2 + yy) * block + first, 16)
        return grads.at[pl.ds(begin, count)]

    def ay(level, other_x):
        xx = 1 - x if other_x else x
        return remote(
            rows(level, xx, 1 - y, 0, large), l_ay.at[level, other_x],
            ay_s.at[level, other_x], ay_r.at[level, other_x], over_y,
        )

    def bx(level, other_y):
        yy = 1 - y if other_y else y
        return remote(
            rows(level, 1 - x, yy, start_b, large), l_bx.at[level, other_y],
            bx_s.at[level, other_y], bx_r.at[level, other_y], over_x,
        )

    def ax(level):
        return remote(l_ay.at[level, 1], l_ax.at[level], ax_s.at[level], ax_r.at[level], over_x)

    def by(level):
        return remote(l_bx.at[level, 1], l_by.at[level], by_s.at[level], by_r.at[level], over_y)

    def fetch(refs):
        copies = []
        first = 0
        for index, ref in enumerate(refs):
            copy = pltpu.make_async_copy(
                ref, stage.at[pl.ds(first, ref.shape[0])], stage_sem.at[index]
            )
            copy.start()
            copies.append(copy)
            first += ref.shape[0]
        return copies

    def add(target, first, count, others, keep=None):
        strip = count
        while strip > 192 or count % strip:
            strip -= 16

        def one(index, carry):
            at = pl.ds(pl.multiple_of(index * strip, 16), strip)
            value = stage[pl.ds(pl.multiple_of(first + index * strip, 16), strip)].astype(F32)
            for ref in [target] + others:
                value = value + ref[at].astype(F32)
            if keep is None:
                target[at] = value.astype(BF16)
            else:
                keep[at] = value
            return carry

        lax.fori_loop(0, count // strip, one, 0)

    def sides(step):
        out = [(z - step, z - step >= 0)]
        if not (isinstance(step, int) and step == 0):
            out.append((z + step, z + step < depth))
        return out

    def backwards(body, first, last):
        if depth <= 4:
            for step in range(first, last - 1, -1):
                body(step)
        else:
            def looped(turn, carry):
                body(first - turn)
                return carry

            lax.fori_loop(0, first - last + 1, looped, 0)

    def leaves(step):
        for level, cond in sides(step):
            def go(level=level):
                for other in (1, 0):
                    ay(level, other).start()
                    bx(level, other).start()

            when(cond, go)

    def zcd(level, way, part):
        device = down if way == 0 else up
        beyond = z + 1 < depth if way == 0 else z >= 1
        at_home = (z - 1 == level) if way == 0 else (z + 1 == level)
        entry = level if way == 0 else level + (depth - level) * at_home.astype(jnp.int32)
        dst = l_zcd.at[entry, part]
        src = rows(level, part // 2, part % 2, start_c, 2 * small)
        send_sem, recv_sem = zcd_s.at[level, part], zcd_r.at[entry, part]
        leaf = remote(src, dst, send_sem, recv_sem, device)
        node = remote(l_zcd.at[level, part], dst, send_sem, recv_sem, device)
        return beyond, leaf, node, src

    def plane_step(step):
        for way, level, cond in ((0, z - step, z - step >= 0), (1, z + step, z + step < depth)):
            def go(way=way, level=level):
                hops = [zcd(level, way, part) for part in range(4)]
                beyond = hops[0][0]

                @pl.when(beyond)
                def _():
                    copies = fetch([hop[3] for hop in hops])
                    for part, (_, leaf, node, src) in enumerate(hops):
                        remote(
                            l_zcd.at[level, part], l_zcd.at[level, part], zcd_s.at[level, part],
                            zcd_r.at[level, part], up,
                        ).wait_recv()
                        copies[part].wait()
                        add(l_zcd.at[level, part], part * 2 * small, 2 * small, [])
                        node.start()

                @pl.when(jnp.logical_not(beyond))
                def _():
                    for _, leaf, node, src in hops:
                        leaf.start()

            when(cond, go)

    def zab(level, way):
        device = down if way == 0 else up
        beyond = z + 1 < depth if way == 0 else z >= 1
        at_home = (z - 1 == level) if way == 0 else (z + 1 == level)
        entry = level if way == 0 else level + (depth - level) * at_home.astype(jnp.int32)
        copies = []
        for index, landing in enumerate((l_ax, l_by)):
            copies.append(
                remote(
                    landing.at[level], l_zab.at[entry, index], zab_s.at[level, index],
                    zab_r.at[entry, index], device,
                )
            )
        return beyond, copies

    def zab_arrived(entry, index):
        remote(
            l_zab.at[entry, index], l_zab.at[entry, index], zab_s.at[entry, index],
            zab_r.at[entry, index], up,
        ).wait_recv()

    def across(level):
        copies = fetch([rows(level, 1 - x, y, 0, large), rows(level, x, 1 - y, start_b, large)])
        ay(level, 1).wait_recv()
        copies[0].wait()
        add(l_ay.at[level, 1], 0, large, [])
        ax(level).start()
        bx(level, 1).wait_recv()
        copies[1].wait()
        add(l_bx.at[level, 1], large, large, [])
        by(level).start()

    def line_step(step):
        for way, level, cond in ((0, z - step, z - step >= 0), (1, z + step, z + step < depth)):
            def go(way=way, level=level):
                copies = fetch([rows(level, x, y, 0, 2 * large)])
                beyond, hops = zab(level, way)
                ay(level, 0).wait_recv()
                ax(level).wait_recv()
                copies[0].wait()

                @pl.when(beyond)
                def _():
                    zab_arrived(level, 0)
                    add(l_ax.at[level], 0, large, [l_ay.at[level, 0], l_zab.at[level, 0]])

                @pl.when(jnp.logical_not(beyond))
                def _():
                    add(l_ax.at[level], 0, large, [l_ay.at[level, 0]])

                hops[0].start()
                bx(level, 0).wait_recv()
                by(level).wait_recv()

                @pl.when(beyond)
                def _():
                    zab_arrived(level, 1)
                    add(l_by.at[level], large, large, [l_bx.at[level, 0], l_zab.at[level, 1]])

                @pl.when(jnp.logical_not(beyond))
                def _():
                    add(l_by.at[level], large, large, [l_bx.at[level, 0]])

                hops[1].start()

            when(cond, go)

    def both(step, action):
        for level, cond in sides(step):
            when(cond, functools.partial(action, level))

    def turn(step):
        leaves(step)
        plane_step(step)
        both(step, across)
        line_step(step)

    backwards(turn, depth - 1, 1)
    leaves(0)

    def home(entry, part, cond):
        def go():
            remote(
                l_zcd.at[entry, part], l_zcd.at[entry, part], zcd_s.at[0, part],
                zcd_r.at[entry, part], up,
            ).wait_recv()

        when(cond, go)

    above, below = z + 1 < depth, z >= 1
    copies = fetch([rows(z, part // 2, part % 2, start_c, 2 * small) for part in range(4)])
    for part in range(4):
        home(z, part, above)
        home(depth, part, below)
        copies[part].wait()

        @pl.when(above & below)
        def _(part=part):
            add(l_zcd.at[z, part], part * 2 * small, 2 * small, [l_zcd.at[depth, part]])

        @pl.when(above & jnp.logical_not(below))
        def _(part=part):
            add(l_zcd.at[z, part], part * 2 * small, 2 * small, [])

        @pl.when(jnp.logical_not(above))
        def _(part=part):
            strip = 2 * small
            value = stage[pl.ds(part * strip, strip)].astype(F32) + l_zcd[depth, part].astype(F32)
            l_zcd[z, part] = value.astype(BF16)

    def block_at(xx, yy, first):
        return l_zcd.at[z, xx * 2 + yy, pl.ds(first, small)]

    plane = [
        remote(block_at(1 - x, 1 - y, 0), l_c.at[1], cd_s.at[0], cd_r.at[0], over_y),
        remote(block_at(x, 1 - y, 0), l_c.at[0], cd_s.at[1], cd_r.at[1], over_y),
        remote(block_at(1 - x, 1 - y, small), l_d.at[1], cd_s.at[2], cd_r.at[2], over_x),
        remote(block_at(1 - x, y, small), l_d.at[0], cd_s.at[3], cd_r.at[3], over_x),
        remote(l_c.at[1], l_c.at[2], cd_s.at[4], cd_r.at[4], over_x),
        remote(l_d.at[1], l_d.at[2], cd_s.at[5], cd_r.at[5], over_y),
    ]
    for copy in plane[:4]:
        copy.start()
    both(0, across)
    plane[0].wait_recv()
    l_c[1] = (l_c[1].astype(F32) + l_zcd[z, (1 - x) * 2 + y, pl.ds(0, small)].astype(F32)).astype(BF16)
    plane[4].start()
    plane[2].wait_recv()
    l_d[1] = (l_d[1].astype(F32) + l_zcd[z, x * 2 + 1 - y, pl.ds(small, small)].astype(F32)).astype(BF16)
    plane[5].start()

    copies = fetch([rows(z, x, y, 0, 2 * large)])
    copies[0].wait()
    for index, (first_hop, second_hop, first_land, second_land, begin) in enumerate(
        ((ay, ax, l_ay, l_ax, 0), (bx, by, l_bx, l_by, start_b))
    ):
        first_hop(z, 0).wait_recv()
        second_hop(z).wait_recv()
        base = [second_land.at[z], first_land.at[z, 0]]
        target = final.at[pl.ds(begin, large)]

        @pl.when(above)
        def _(index=index):
            zab_arrived(z, index)

        @pl.when(below)
        def _(index=index):
            zab_arrived(depth, index)

        for cond, more in (
            (above & below, [z, depth]),
            (above & jnp.logical_not(below), [z]),
            (jnp.logical_not(above), [depth]),
        ):
            @pl.when(cond)
            def _(more=more, base=base, target=target, begin=begin, index=index):
                add(
                    base[0], begin, large,
                    base[1:] + [l_zab.at[entry, index] for entry in more], keep=target,
                )

    for copy in (plane[1], plane[3], plane[4], plane[5]):
        copy.wait_recv()
    here = x * 2 + y
    final[pl.ds(start_c, small)] = (
        l_zcd[z, here, pl.ds(0, small)].astype(F32) + l_c[0].astype(F32) + l_c[2].astype(F32)
    )
    final[pl.ds(start_d, small)] = (
        l_zcd[z, here, pl.ds(small, small)].astype(F32) + l_d[0].astype(F32) + l_d[2].astype(F32)
    )
    own_rows = block // 2
    theirs = final.at[pl.ds(pl.multiple_of((1 - core) * own_rows, 16), own_rows)]
    mine = final.at[pl.ds(pl.multiple_of(core * own_rows, 16), own_rows)]
    cross = remote(theirs, result, swap_s.at[0], swap_r.at[0], place.partner())
    cross.start()
    local = pltpu.make_async_copy(mine, out.at[core], out_sem.at[0])
    local.start()

    def drain(step):
        for level, cond in sides(step):
            def go(level=level):
                for other in range(2):
                    ay(level, other).wait_send()
                    bx(level, other).wait_send()
                ax(level).wait_send()
                by(level).wait_send()

            when(cond, go)
        if not (isinstance(step, int) and step == 0):
            for way, level, cond in ((0, z - step, z - step >= 0), (1, z + step, z + step < depth)):
                def go(way=way, level=level):
                    for part in range(4):
                        zcd(level, way, part)[2].wait_send()
                    for copy in zab(level, way)[1]:
                        copy.wait_send()

                when(cond, go)

    steps(depth, drain)
    for copy in plane:
        copy.wait_send()
    cross.wait()
    fetched = pltpu.make_async_copy(result, out.at[1 - core], out_sem.at[1])
    fetched.start()
    fetched.wait()
    local.wait()


def run_reduce(depth, block, grads):
    half = grads.shape[1]
    large, small = cut(block, 16)
    dma = pltpu.SemaphoreType.DMA
    anywhere = pl.BlockSpec(memory_space=pl.ANY)
    scratch = [
        pltpu.VMEM((depth, 2, large, half), BF16),
        pltpu.VMEM((depth, large, half), BF16),
        pltpu.VMEM((depth, 2, large, half), BF16),
        pltpu.VMEM((depth, large, half), BF16),
        pltpu.VMEM((depth + 1, 2, large, half), BF16),
        pltpu.VMEM((depth + 1, 4, 2 * small, half), BF16),
        pltpu.VMEM((3, small, half), BF16),
        pltpu.VMEM((3, small, half), BF16),
        pltpu.VMEM((max(2 * large, 8 * small), half), BF16),
        pltpu.VMEM((block, half), F32),
        pltpu.VMEM((block // 2, half), F32),
        dma((4,)), dma((2,)), dma((1,)), dma((1,)),
        dma((depth, 2)), dma((depth, 2)), dma((depth,)), dma((depth,)),
        dma((depth, 2)), dma((depth, 2)), dma((depth,)), dma((depth,)),
        dma((depth + 1, 2)), dma((depth + 1, 2)),
        dma((depth + 1, 4)), dma((depth + 1, 4)),
        dma((6,)), dma((6,)),
    ]
    return pl.pallas_call(
        functools.partial(reduce_kernel, depth, block),
        out_shape=jax.ShapeDtypeStruct((2, block // 2, half), F32),
        in_specs=[anywhere],
        out_specs=anywhere,
        scratch_shapes=scratch,
        compiler_params=pltpu.CompilerParams(
            collective_id=2, has_side_effects=True, vmem_limit_bytes=62 << 20
        ),
        name="reduce",
    )(grads)


def adamw(gradient, params, first_moment, second_moment, rate, decay):
    moment_new = beta_one * first_moment + (1.0 - beta_one) * gradient
    second_new = beta_two * second_moment + (1.0 - beta_two) * gradient * gradient
    direction = (
        moment_new
        / (1.0 - beta_one**STEP)
        / (jnp.sqrt(second_new / (1.0 - beta_two**STEP)) + adam_eps)
    )
    return (moment_new, second_new, params - rate * (direction + decay * params))


def update_kernel(
    filled_ref, sums_ref, master_ref, one_ref, two_ref, average_ref,
    grad_ref, one_out, two_out, new_ref, average_out, copy_ref,
):
    filled = filled_ref[pl.program_id(0)] > 0
    half = sums_ref.shape[2]
    strip = 32

    def one(index, carry):
        at = pl.ds(pl.multiple_of(index * strip, strip), strip)
        for h in range(2):
            lanes = pl.ds(h * half, half)
            gradient = jnp.where(filled, sums_ref[h, at], 0.0)
            master = master_ref[at, lanes]
            moment, second, new = adamw(
                gradient, master, one_ref[at, lanes], two_ref[at, lanes], rate_main, decay_main
            )
            grad_ref[at, lanes] = gradient
            one_out[at, lanes] = moment
            two_out[at, lanes] = second
            new_ref[at, lanes] = new
            average_out[at, lanes] = ema_keep * average_ref[at, lanes] + (1.0 - ema_keep) * new
            copy_ref[at, lanes] = new.astype(BF16)
        return carry

    lax.fori_loop(0, master_ref.shape[0] // strip, one, 0)


def run_update(filled, sums, master, moment_one, moment_two, average):
    rows, width = master.shape
    step = rows // filled.shape[0]
    spec = pl.BlockSpec((step, width), lambda i, t: (i, 0))
    grid_spec = pltpu.PrefetchScalarGridSpec(
        num_scalar_prefetch=1,
        grid=(rows // step,),
        in_specs=[pl.BlockSpec((2, step, sums.shape[2]), lambda i, t: (0, i, 0))] + [spec] * 4,
        out_specs=[spec] * 6,
    )
    full = jax.ShapeDtypeStruct(master.shape, F32)
    return pl.pallas_call(
        update_kernel,
        grid_spec=grid_spec,
        out_shape=[full] * 5 + [jax.ShapeDtypeStruct(master.shape, BF16)],
        compiler_params=pltpu.CompilerParams(vmem_limit_bytes=60 << 20),
        name="update",
    )(filled, sums, master, moment_one, moment_two, average)


def body(
    inputs,
    dense_inputs,
    lengths,
    owners,
    cotangent,
    master,
    moment_one,
    moment_two,
    average,
    norm_gain,
    norm_shift,
    norm_one,
    norm_two,
):
    width = inputs.shape[2]
    wides, narrows = lax.axis_size("wide"), lax.axis_size("narrow")
    depth = wides // 2
    own_rows = master.shape[0]
    block = 2 * own_rows
    capacity = own_rows * narrows // width
    places = slot_table(owners, capacity)
    act, dcv, res, block_out, input_grad, dense_grad, sums = run_chain(
        depth, block, places, lengths, master, inputs, dense_inputs, cotangent, norm_gain, norm_shift
    )
    owner = places // capacity
    compact = ((owner // 4) * 2 + owner % 2) * capacity + places % capacity
    parity = (lax.axis_index("wide") // 2) % 2
    handled = jnp.where((owner // 2) % 2 == parity, compact, -1).astype(jnp.int32)
    grads = run_grads(wides * narrows * own_rows // 2, handled, act, dcv, res)
    reduced = run_reduce(depth // 2, block, grads)

    step = min(own_rows, 256)
    first = (lax.axis_index("wide") * narrows + lax.axis_index("narrow")) * own_rows
    slot_of_step = (first + step * jnp.arange(own_rows // step, dtype=jnp.int32)) // width
    filled = jnp.any(places[None, :] == slot_of_step[:, None], axis=1).astype(jnp.int32)
    updated = run_update(filled, reduced, master, moment_one, moment_two, average)
    sums = sums.transpose(1, 0, 2).reshape(sums.shape[1], -1)
    branches = SUBS + SOURCES
    shift_rows = sums[branches : branches + SUBS]
    norm_grad = jnp.stack(
        [
            sums[:branches],
            jnp.concatenate([shift_rows] + [shift_rows[SUBS - 1 :]] * SOURCES, axis=0),
        ]
    )
    norm_params = jnp.stack([norm_gain, norm_shift])
    norm_one_new, norm_two_new, norm_new = adamw(
        norm_grad, norm_params, norm_one, norm_two, rate_norm, 0.0
    )
    return (
        block_out,
        input_grad,
        dense_grad,
        *updated,
        norm_grad,
        norm_one_new,
        norm_two_new,
        norm_new,
    )


def solution(mesh):
    rows = P(AXES, None)
    utterances = P(AXES, None, None)
    in_specs = (
        utterances, utterances, P(AXES), P(), utterances, rows, rows, rows, rows,
        P(), P(), P(), P(),
    )
    out_specs = (
        utterances, utterances, utterances, rows, rows, rows, rows, rows, rows,
        P(), P(), P(), P(),
    )
    return jax.shard_map(body, mesh=mesh, in_specs=in_specs, out_specs=out_specs, check_vma=False)
```

profile of v0, /device:TPU:0, one launch (start us, length us, event | category | flops | bytes accessed | tf_op | source)
XLA Modules:
  0.0 487.4 jit_solution(15822252294519891303)
XLA Ops:
  0.7 0.9 select_reduce_fusion
  1.6 1.2 compare_select_fusion.2
  3.4 0.0 copy-start.8
  3.5 326.1 %chain.1 = (bf16[5,2,2,2,256,256]{5,4,3,2,1,0:T(8,128)(2,1)}, bf16[5,2,2,288,256]{4,3,2,1,0:T(8,128)(2,1)}, bf16[2,4,512,256]{3,2,1,0:T(8,128)(2,1)}, bf16[1,256...) custom-call(s32[89]{0:T(128)} %get-tuple-element.69.slot_ref, ...), custom_call_target="tpu_custom_call" | custom-call | flops 22817013760 | bytes 16777216 | tf_op jit(solution)/shard_map/chain/pallas_call | solution.py:915
  329.6 0.0 copy-done.8
  329.6 0.2 compare_reduce_fusion
  329.8 0.5 convert_element_type.3.filled_ref
  330.3 26.5 %weight_grads.1.grads = bf16[24576,256]{1,0:T(8,128)(2,1)} custom-call(s32[89]{0:T(128)} %get-tuple-element.68.slot_ref, bf16[5,2,2,2,256,256]{5,4,3,2,1,0:T(8,128)(2,1)} %get-tuple-element.29.act_ref, bf16[5,2,2,288,256]{4,3,2,1,0:T(8,128)(2,1)} %get-tuple-element.30.dcv_ref, bf16[2,4,512,256]{3,2,1,0:T(8,128)(2,1)} %get-tuple-element.31.res_ref), custom_call_target="tpu_custom_call" | custom-call | tf_op jit(solution)/shard_map/weight_grads/pallas_call | solution.py:1014
  356.8 110.9 %reduce.1.sums_ref = f32[2,1536,256]{2,1,0:T(8,128)} custom-call(bf16[24576,256]{1,0:T(8,128)(2,1)} %weight_grads.1.grads), custom_call_target="tpu_custom_call" | custom-call | tf_op jit(solution)/shard_map/reduce/pallas_call | solution.py:1384
  467.8 0.0 copy-start.3
  467.8 0.0 copy-start.4
  467.8 0.0 copy-start.5
  467.8 0.0 copy-start.6
  467.8 0.0 copy-start.7
  467.8 0.0 copy-start.2
  467.8 0.0 copy-start.1
  467.9 14.1 %update.1 = (f32[1536,512]{1,0:T(8,128)}, f32[1536,512]{1,0:T(8,128)}, f32[1536,512]{1,0:T(8,128)}, f32[1536,512]{1,0:T(8,128)}, f32[1536,512]{1,0:T(8,128)}, /*index=5*/bf16[1536,512]{1,0:T(8,128)(2,1)}) custom-call(s32[6]{0:T(128)} %convert_element_type.3.filled_ref, f32[2,1536,256]{2,1,0:T(8,128)} %reduce.1.sums_ref, f32[1536,512]{1,0:T(8,128)} %master_ref.1, ...), custom_call_target="tpu_custom_call" | custom-call | tf_op jit(solution)/shard_map/update/pallas_call | solution.py:1447
  481.9 0.0 copy-done.3
  481.9 0.1 concatenate.3
  482.1 0.0 copy-done.4
  482.1 0.0 copy-done.5
  482.1 0.0 copy-done.6
  482.1 0.0 copy-done.7
  482.1 0.1 multiply_subtract_fusion
  482.2 0.7 copy.36
  482.8 0.7 copy.37
  483.5 0.7 copy.38
  484.1 0.7 copy.39
  484.8 0.7 copy.52
  485.5 0.8 copy.53
  486.3 0.0 copy-done
  486.3 1.1 copy.54
  (8 shorter events, 0.1 us)
Async XLA Ops:
  3.4 326.2 %copy-start.8 = (s32[89]{0:T(128)S(1)}, s32[89]{0:T(128)}, u32[]{:S(2)}) copy-start(s32[89]{0:T(128)} %get-tuple-element.69.slot_ref) | copy-start | bytes 1072
  467.8 14.1 %copy-start.3 = (f32[2,16,256]{2,1,0:T(8,128)S(1)}, f32[2,16,256]{2,1,0:T(8,128)}, u32[]{:S(2)}) copy-start(f32[2,16,256]{2,1,0:T(8,128)} %get-tuple-element.38) | copy-start | bytes 98308
  467.8 14.3 %copy-start.4 = (f32[2,11,512]{2,0,1:T(2,128)S(1)}, f32[2,11,512]{2,0,1:T(2,128)}, u32[]{:S(2)}) copy-start(f32[2,11,512]{2,0,1:T(2,128)} %param.25) | copy-start | bytes 135172
  467.8 14.3 %copy-start.5 = (f32[2,11,512]{2,0,1:T(2,128)S(1)}, f32[2,11,512]{2,0,1:T(2,128)}, u32[]{:S(2)}) copy-start(f32[2,11,512]{2,0,1:T(2,128)} %param.24) | copy-start | bytes 135172
  467.8 14.3 %copy-start.6 = (f32[11,512]{1,0:T(8,128)S(1)}, f32[11,512]{1,0:T(8,128)}, u32[]{:S(2)}) copy-start(f32[11,512]{1,0:T(8,128)} %gain_ref.1) | copy-start | bytes 67588
  467.8 14.3 %copy-start.7 = (f32[11,512]{1,0:T(8,128)S(1)}, f32[11,512]{1,0:T(8,128)}, u32[]{:S(2)}) copy-start(f32[11,512]{1,0:T(8,128)} %shift_ref.1) | copy-start | bytes 67588
  467.8 17.0 %copy-start.2 = (bf16[1,256,512]{2,1,0:T(8,128)(2,1)S(1)}, bf16[1,256,512]{2,1,0:T(8,128)(2,1)}, u32[]{:S(2)}) copy-start(bf16[1,256,512]{2,1,0:T(8,128)(2,1)} %get-tuple-element.84) | copy-start | bytes 786436
  467.8 17.7 %copy-start.1 = (f32[1,256,512]{2,1,0:T(8,128)S(1)}, f32[1,256,512]{2,1,0:T(8,128)}, u32[]{:S(2)}) copy-start(f32[1,256,512]{2,1,0:T(8,128)} %get-tuple-element.85) | copy-start | bytes 1572868
  481.9 4.4 copy-start
where the time goes:
time: 487 us
  Pallas kernels  478 us (98%)
  local copies, waits for them, and re-layouts  5.41 us (1%)
    pallas_call x1, Pallas kernels, run_chain(): pl.pallas_call(functools.partial(chain_kernel, depth, block), out_shape=o...  326 us
    pallas_call x1, Pallas kernels, run_reduce(): pl.pallas_call(functools.partial(reduce_kernel, depth, block), out_shape=...  111 us
    pallas_call x1, Pallas kernels, run_grads(): pl.pallas_call(grad_kernel, grid_spec=grid_spec, out_shape=jax.ShapeDtype...  26.5 us
    pallas_call x1, Pallas kernels, run_update(): pl.pallas_call(update_kernel, grid_spec=grid_spec, out_shape=[full] * 5 +...  14.1 us

commit v1 on v0

--- a/solution.py
+++ b/solution.py
@@ -177,7 +177,7 @@
     ]
 
 
-def gather_bank(place, bank, block, sems, meanwhile=lambda: None):
+def gather_bank(place, bank, block, sems, first_idle=lambda: None, second_idle=lambda: None):
     depth, z, x, y = place.depth, place.z, place.x, place.y
     large, small = cut(block, 9)
     (zab_s, zab_r, zcd_s, zcd_r, ax_s, ax_r, ay_s, ay_r, by_s, by_r, bx_s, bx_r, cd_s, cd_r) = sems
@@ -261,12 +261,10 @@
             def begin(level=level):
                 ax(level).start()
                 by(level).start()
-                ay(level, 0).start()
-                bx(level, 0).start()
 
             when(cond, begin)
         if isinstance(step, int) and step == 0:
-            meanwhile()
+            first_idle()
             plane[2].start()
             plane[4].start()
             plane[0].wait_recv()
@@ -279,12 +277,16 @@
                 when(cond, copy.start)
         for level, cond in sides(step):
             def across(level=level):
+                ay(level, 0).start()
+                bx(level, 0).start()
                 ax(level).wait_recv()
                 ay(level, 1).start()
                 by(level).wait_recv()
                 bx(level, 1).start()
 
             when(cond, across)
+        if isinstance(step, int) and step == 0:
+            second_idle()
         if not (isinstance(step, int) and step == 0):
             for level, cond in sides(step):
                 def arrived(level=level):
@@ -327,7 +329,7 @@
     def one(index, carry):
         return body(pl.ds(pl.multiple_of(index * strip, strip), strip), carry)
 
-    return lax.fori_loop(0, rows // strip, one, carry)
+    return lax.fori_loop(0, rows // strip, one, carry, unroll=True)
 
 
 def fold(values):
@@ -338,9 +340,9 @@
     depth, block,
     slot_ref, length_ref, master, own_x, own_dense, own_cot, gain_ref, shift_ref,
     act_out, dcv_out, res_out, blk_out, ig_out, dg_out, nrm_out,
-    bank, act, dense, mask, cot, raw, side, pre4, slope, upown, upsend, uprecv, dcv, dsd, res, dgrecv,
-    igrecv, stage, nrm, blk, blksend, keep, ex_side, ex_last, ex_sub,
-    load_sem, swap_s, swap_r, act_s, act_r, up_s, up_r, ex_s, ex_r, out_sem, far_s, far_r, near_s, near_r,
+    bank, act, dense, mask, cot, raw, side, pre4, slope, upown, upsend, uprecv, dcv, dsd, res, res_x, res_y, dgrecv,
+    igrecv, stage, turned, nrm, blk, blksend, keep, ex_side, ex_last, ex_sub,
+    load_sem, swap_s, swap_r, act_s, act_r, up_s, up_r, ex_s, ex_r, out_sem, far_s, far_r, near_s, near_r, own_sem,
     *tree,
 ):
     place = Place(depth)
@@ -436,10 +438,43 @@
             copy.start()
         return swaps
 
+    def own_act(section):
+        half_of = turned.at[lax.rem(section, 2)]
+        return [
+            pltpu.make_async_copy(half_of, act_out.at[section, 0, core], own_sem.at[section]),
+            remote(
+                half_of, act_out.at[section, 0, core], near_s.at[section], near_r.at[section], partner
+            ),
+            remote(
+                half_of, act_out.at[section, 1, core], far_s.at[section], far_r.at[section], beside
+            ),
+        ]
+
+    def pass_act(section):
+        ref = act_out.at[section, 1, core]
+        return remote(ref, ref, near_s.at[SUBS + section], near_r.at[SUBS + section], partner)
+
+    def turn_act(section):
+        turned[lax.rem(section, 2)] = jnp.concatenate(
+            [act[section, core, u, inner] for u in range(2)], axis=0
+        ).T
+        for copy in own_act(section):
+            copy.start()
+
+    def free_turned(section):
+        copies = own_act(section)
+        copies[0].wait()
+        copies[1].wait_send()
+        copies[2].wait_send()
+
     swaps = []
-    gather_bank(place, bank, block, tree, lambda: swaps.extend(prepare()))
-    for copy in swaps:
-        copy.wait()
+
+    def arrived():
+        for copy in swaps:
+            copy.wait()
+        turn_act(0)
+
+    gather_bank(place, bank, block, tree, lambda: swaps.extend(prepare()), arrived)
 
     outs = []
 
@@ -447,16 +482,6 @@
         copy = pltpu.make_async_copy(src, dst, out_sem.at[len(outs)])
         copy.start()
         outs.append(copy)
-
-    def far_act(section):
-        return remote(
-            act.at[section, core, :, inner], act_out.at[section, 1, core],
-            far_s.at[section], far_r.at[section], beside,
-        )
-
-    def near_act(section):
-        ref = act_out.at[section, 1, core]
-        return remote(ref, ref, near_s.at[section], near_r.at[section], partner)
 
     def far_dcv(section):
         return remote(
@@ -464,13 +489,20 @@
             far_s.at[SUBS + section], far_r.at[SUBS + section], beside,
         )
 
-    def far_res(index):
-        return remote(
-            res.at[index], res_out.at[1, index],
-            far_s.at[2 * SUBS + index], far_r.at[2 * SUBS + index], beside,
+    def keep_dcv(section):
+        return pltpu.make_async_copy(
+            dcv.at[section], dcv_out.at[section, 0], own_sem.at[SUBS + section]
         )
 
-    far_act(0).start()
+    def res_over(step):
+        if step == 0:
+            src, dst, device = res.at[pl.ds(2 * (1 - place.x), 2)], res_x, place.over_x()
+        elif step == 1:
+            src, dst, device = res_x.at[1 - place.y], res_y, place.over_y()
+        else:
+            src, dst, device = res_y, res_out.at[1], beside
+        at = 2 * SUBS + step
+        return remote(src, dst, far_s.at[at], far_r.at[at], device)
 
     def weight(matrix, first, count):
         begin = slot_ref[matrix] * (width // UNIT) + first // UNIT
@@ -601,6 +633,20 @@
         total, square = moments(lambda at: raw[section, at], count)
         buffer = ex_sub.at[lax.rem(section, 2)]
         share(buffer, 1 + section, jnp.concatenate([count, total, square, jnp.zeros_like(count)], axis=0))
+
+        def background():
+            own_act(section - 1)[2].wait_recv()
+            pass_act(section - 1).start()
+            if isinstance(section, int):
+                free_turned(section - 2)
+            else:
+                pl.when(section > 1)(functools.partial(free_turned, section - 2))
+            turn_act(section)
+
+        if isinstance(section, int):
+            background()
+        else:
+            pl.when(section > 0)(background)
         parts = shared(buffer, 1 + section)
         mean, inverse, frame_total = merge(parts[:, 0], parts[:, 1], parts[:, 2])
         save(section, mean, inverse)
@@ -629,9 +675,6 @@
         strips(rows, activate)
         if not last:
             swap_act(section + 1).start()
-            far_act(section + 1).start()
-            far_act(section).wait_recv()
-            near_act(section).start()
         return frame_total
 
     def looped(section, carry):
@@ -665,10 +708,8 @@
     blk_copy.start()
     for section in range(1, SUBS):
         swap_act(section).wait_send()
-    for h in range(2):
-        put(act.at[:, h, :, inner], act_out.at[:, 0, h])
-    far_act(SUBS - 1).wait_recv()
-    near_act(SUBS - 1).start()
+    for section in (SUBS - 2, SUBS - 1):
+        free_turned(section)
 
     def hat_of(values, index):
         return values * kept(0, index) - kept(1, index)
@@ -732,6 +773,7 @@
 
         branch(lambda at: raw[section, at], section, shift_sum, gain_sum, store)
         far_dcv(section).start()
+        keep_dcv(section).start()
 
     def cot_at(at):
         return cot[
@@ -790,6 +832,20 @@
                 turned, dsd[SOURCES - 1], preferred_element_type=F32
             ).astype(BF16)
 
+    dg_puts = [
+        pltpu.make_async_copy(
+            dgrecv.at[chunk], dg_out.at[0, :, pl.ds(chunk * half, half)], load_sem.at[chunk]
+        )
+        for chunk in range(chunks)
+    ]
+
+    def finish_dense():
+        dg_copy.wait()
+        own_valid = jnp.concatenate([mask[core]] * (half // 128), axis=1)
+        for chunk in range(chunks):
+            dgrecv[chunk] = (dgrecv[chunk] + side[chunk, pl.ds(ours, frames)]) * own_valid
+            dg_puts[chunk].start()
+
     def looped_back(turn, carry):
         section = SUBS - 2 - turn
         copy = up_copy(section + 1)
@@ -807,10 +863,27 @@
         @pl.when(section == SUBS - 2)
         def _():
             residual_grads()
+            res_over(0).start()
             dense_grads()
 
+        @pl.when(section == SUBS - 3)
+        def _():
+            res_over(0).wait_recv()
+            for index in range(2):
+                total = res[2 * place.x + index].astype(F32) + res_x[index].astype(F32)
+                res_x[index] = total.astype(BF16)
+            res_over(1).start()
+            finish_dense()
+            own_act(SUBS - 1)[2].wait_recv()
+            pass_act(SUBS - 1).start()
+
+        @pl.when(section == SUBS - 4)
+        def _():
+            res_over(1).wait_recv()
+            res_y[...] = (res_y[...].astype(F32) + res_x[place.y].astype(F32)).astype(BF16)
+
         sums = jnp.sum(shared(buffer, SUBS + 2 + section), axis=0)
-        far_res(turn).start()
+        pl.when(section == SUBS - 4)(lambda: res_over(2).start())
         conv_branch(section, sums[0:1], sums[1:2])
         nrm[core, pl.ds(section, 1)] = sums[1:2]
         nrm[core, pl.ds(SUBS + SOURCES + section, 1)] = sums[0:1]
@@ -822,8 +895,7 @@
         return carry
 
     lax.fori_loop(0, SUBS - 1, looped_back, 0)
-    put(dcv, dcv_out.at[:, 0])
-    put(res, res_out.at[0])
+    put(res_y, res_out.at[0])
     nrm_copy = remote(nrm.at[core], nrm.at[core], swap_s.at[7], swap_r.at[7], partner)
     nrm_copy.start()
     for h in range(2):
@@ -835,10 +907,6 @@
     )
     ig_copy.start()
     own_valid = jnp.concatenate([mask[core]] * (half // 128), axis=1)
-    dg_copy.wait()
-    for chunk in range(chunks):
-        dgrecv[chunk] = (dgrecv[chunk] + side[chunk, pl.ds(ours, frames)]) * own_valid
-        put(dgrecv.at[chunk], dg_out.at[0, :, pl.ds(chunk * half, half)])
     blk_copy.wait()
     nrm_copy.wait()
     put(nrm, nrm_out)
@@ -848,12 +916,14 @@
         put(igrecv.at[h], ig_out.at[0, :, pl.ds(h * half, half)])
         put(blk.at[h], blk_out.at[0, :, pl.ds(h * half, half)])
     for section in range(SUBS):
-        near_act(section).wait()
-        far_act(section).wait_send()
+        own_act(section)[1].wait_recv()
+        pass_act(section).wait()
         far_dcv(section).wait()
-    for index in range(4):
-        far_res(index).wait()
-    for copy in outs:
+        keep_dcv(section).wait()
+    res_over(0).wait_send()
+    res_over(1).wait_send()
+    res_over(2).wait()
+    for copy in outs + dg_puts:
         copy.wait()
 
 
@@ -869,9 +939,9 @@
     vmem = pl.BlockSpec(memory_space=pltpu.VMEM)
     smem = pl.BlockSpec(memory_space=pltpu.SMEM)
     out_shape = [
-        jax.ShapeDtypeStruct((SUBS, 2, 2, 2, frames, half), BF16),
+        jax.ShapeDtypeStruct((SUBS, 2, 2, half, rows), BF16),
         jax.ShapeDtypeStruct((SUBS, 2, 2, padded, half), BF16),
-        jax.ShapeDtypeStruct((2, 4, width, half), BF16),
+        jax.ShapeDtypeStruct((2, width, half), BF16),
         jax.ShapeDtypeStruct(x.shape, BF16),
         jax.ShapeDtypeStruct(x.shape, F32),
         jax.ShapeDtypeStruct(dense.shape, F32),
@@ -893,9 +963,12 @@
         pltpu.VMEM((SUBS, 2, padded, half), BF16),
         pltpu.VMEM((SOURCES, rows, half), BF16),
         pltpu.VMEM((4, width, half), BF16),
+        pltpu.VMEM((2, width, half), BF16),
+        pltpu.VMEM((width, half), BF16),
         pltpu.VMEM((chunks, frames, half), F32),
         pltpu.VMEM((2, frames, half), F32),
         pltpu.VMEM((block // 2 // UNIT, UNIT, half), BF16),
+        pltpu.VMEM((2, half, rows), BF16),
         pltpu.VMEM((2, 16, half), F32),
         pltpu.VMEM((2, frames, half), BF16),
         pltpu.VMEM((frames, half), BF16),
@@ -909,8 +982,9 @@
         dma((2,)), dma((2,)),
         dma((2 * SUBS + 1,)), dma((2 * SUBS + 1,)),
         dma((10 + chunks,)),
-        dma((2 * SUBS + 4,)), dma((2 * SUBS + 4,)),
-        dma((SUBS,)), dma((SUBS,)),
+        dma((2 * SUBS + 3,)), dma((2 * SUBS + 3,)),
+        dma((2 * SUBS,)), dma((2 * SUBS,)),
+        dma((2 * SUBS,)),
     ] + tree_sems(depth)
     return pl.pallas_call(
         functools.partial(chain_kernel, depth, block),
@@ -928,18 +1002,12 @@
     )(places, lengths, master, x, dense, cot, gains, shifts)
 
 
-def grad_kernel(slot_ref, act_ref, dcv_ref, res_ref, out_ref, left, stage, count, sems):
+def grad_kernel(slot_ref, act_ref, dcv_ref, res_ref, out_ref, stage, count, sems):
     section = pl.program_id(0)
-    half = act_ref.shape[5]
+    half = act_ref.shape[3]
     width = 2 * half
-    frames = act_ref.shape[4]
-    rows = 2 * frames
+    frames = act_ref.shape[4] // 2
     ring = stage.shape[0]
-    for pair in range(2):
-        for h in range(2):
-            left[pl.ds(h * half, half), pl.ds(pair * rows, rows)] = (
-                act_ref[0, pair, h].reshape(rows, half).T
-            )
 
     @pl.when(section == 0)
     def _():
@@ -963,24 +1031,27 @@
 
     for k in range(K):
         def conv(k=k):
-            right = jnp.concatenate(
-                [
-                    dcv_ref[0, pair, u, pl.ds(EDGE + MARGIN - k, frames)]
-                    for pair in range(2)
-                    for u in range(2)
-                ],
-                axis=0,
-            )
-            return jnp.dot(left[...], right, preferred_element_type=F32)
+            total = None
+            for pair in range(2):
+                right = jnp.concatenate(
+                    [dcv_ref[0, pair, u, pl.ds(EDGE + MARGIN - k, frames)] for u in range(2)], axis=0
+                )
+                left = act_ref[0, pair].reshape(width, 2 * frames)
+                term = jnp.dot(left, right, preferred_element_type=F32)
+                total = term if total is None else total + term
+            return total
 
         emit(section * K + k, conv)
 
     @pl.when(section == SUBS - 1)
     def _():
         for index in range(4):
+            here = slot_ref[SUBS * K + 4] == index
             emit(
                 SUBS * K + index,
-                lambda index=index: res_ref[0, index].astype(F32) + res_ref[1, index].astype(F32),
+                lambda here=here: jnp.where(
+                    here, res_ref[0].astype(F32) + res_ref[1].astype(F32), 0.0
+                ),
             )
         turns = count[0]
 
@@ -992,20 +1063,18 @@
 
 
 def run_grads(total_rows, places, act, dcv, res):
-    half = act.shape[5]
-    frames = act.shape[4]
+    half = act.shape[3]
     ring = 8
     grid_spec = pltpu.PrefetchScalarGridSpec(
         num_scalar_prefetch=1,
         grid=(SUBS,),
         in_specs=[
-            pl.BlockSpec((1,) + act.shape[1:], lambda s, t: (s, 0, 0, 0, 0, 0)),
+            pl.BlockSpec((1,) + act.shape[1:], lambda s, t: (s, 0, 0, 0, 0)),
             pl.BlockSpec((1,) + dcv.shape[1:], lambda s, t: (s, 0, 0, 0, 0)),
-            pl.BlockSpec(res.shape, lambda s, t: (0, 0, 0, 0)),
+            pl.BlockSpec(res.shape, lambda s, t: (0, 0, 0)),
         ],
         out_specs=pl.BlockSpec(memory_space=pl.ANY),
         scratch_shapes=[
-            pltpu.VMEM((2 * half, 4 * frames), BF16),
             pltpu.VMEM((ring, 2 * half, half), BF16),
             pltpu.SMEM((1,), jnp.int32),
             pltpu.SemaphoreType.DMA((ring,)),
@@ -1020,9 +1089,22 @@
     )(places, act, dcv, res)
 
 
+def shares(rows, number):
+    units = rows // UNIT
+    out = []
+    first = 0
+    for index in range(number):
+        count = units // number + (1 if index < units % number else 0)
+        if count:
+            out.append((first * UNIT, count * UNIT))
+        first += count
+    return out
+
+
 def reduce_kernel(
-    depth, block, grads, out, l_ay, l_ax, l_bx, l_by, l_zab, l_zcd, l_c, l_d, stage, final, result,
-    stage_sem, out_sem, swap_s, swap_r, ay_s, ay_r, ax_s, ax_r, bx_s, bx_r, by_s, by_r,
+    depth, block, grads, out, l_ay, l_ax, l_bx, l_by, l_zab, l_zcd, l_c, l_d,
+    o_cross, o_line, o_plane, final, result,
+    cross_sem, line_sem, plane_sem, out_sem, swap_s, swap_r, ay_s, ay_r, ax_s, ax_r, bx_s, bx_r, by_s, by_r,
     zab_s, zab_r, zcd_s, zcd_r, cd_s, cd_r,
 ):
     place = QuadPlace(depth)
@@ -1030,53 +1112,72 @@
     large, small = cut(block, 16)
     start_b, start_c, start_d = large, 2 * large, 2 * large + small
     over_x, over_y, up, down = place.over_x(), place.over_y(), place.up(), place.down()
-    place.enter()
+    pieces = shares(large, 2)
+    runs = range(len(pieces))
 
     def rows(zz, xx, yy, first, count):
         begin = pl.multiple_of(((zz * 2 + xx) * 2 + yy) * block + first, 16)
         return grads.at[pl.ds(begin, count)]
 
-    def ay(level, other_x):
+    def part(run):
+        return pl.ds(*pieces[run])
+
+    def ay(level, other_x, run):
         xx = 1 - x if other_x else x
+        first, count = pieces[run]
         return remote(
-            rows(level, xx, 1 - y, 0, large), l_ay.at[level, other_x],
-            ay_s.at[level, other_x], ay_r.at[level, other_x], over_y,
+            rows(level, xx, 1 - y, first, count), l_ay.at[level, other_x, part(run)],
+            ay_s.at[level, other_x, run], ay_r.at[level, other_x, run], over_y,
         )
 
-    def bx(level, other_y):
+    def bx(level, other_y, run):
         yy = 1 - y if other_y else y
+        first, count = pieces[run]
         return remote(
-            rows(level, 1 - x, yy, start_b, large), l_bx.at[level, other_y],
-            bx_s.at[level, other_y], bx_r.at[level, other_y], over_x,
+            rows(level, 1 - x, yy, start_b + first, count), l_bx.at[level, other_y, part(run)],
+            bx_s.at[level, other_y, run], bx_r.at[level, other_y, run], over_x,
         )
 
-    def ax(level):
-        return remote(l_ay.at[level, 1], l_ax.at[level], ax_s.at[level], ax_r.at[level], over_x)
-
-    def by(level):
-        return remote(l_bx.at[level, 1], l_by.at[level], by_s.at[level], by_r.at[level], over_y)
-
-    def fetch(refs):
-        copies = []
-        first = 0
-        for index, ref in enumerate(refs):
-            copy = pltpu.make_async_copy(
-                ref, stage.at[pl.ds(first, ref.shape[0])], stage_sem.at[index]
+    def ax(level, run):
+        return remote(
+            l_ay.at[level, 1, part(run)], l_ax.at[level, part(run)],
+            ax_s.at[level, run], ax_r.at[level, run], over_x,
+        )
+
+    def by(level, run):
+        return remote(
+            l_bx.at[level, 1, part(run)], l_by.at[level, part(run)],
+            by_s.at[level, run], by_r.at[level, run], over_y,
+        )
+
+    def own_cross(level):
+        return [
+            pltpu.make_async_copy(rows(level, 1 - x, y, 0, large), o_cross.at[level, 0], cross_sem.at[level, 0]),
+            pltpu.make_async_copy(rows(level, x, 1 - y, start_b, large), o_cross.at[level, 1], cross_sem.at[level, 1]),
+        ]
+
+    def own_line(level):
+        return [
+            pltpu.make_async_copy(rows(level, x, y, index * large, large), o_line.at[level, index], line_sem.at[level, index])
+            for index in range(2)
+        ]
+
+    def own_plane(level):
+        return [
+            pltpu.make_async_copy(
+                rows(level, index // 2, index % 2, start_c, 2 * small),
+                o_plane.at[level, index], plane_sem.at[level, index],
             )
-            copy.start()
-            copies.append(copy)
-            first += ref.shape[0]
-        return copies
-
-    def add(target, first, count, others, keep=None):
-        strip = count
-        while strip > 192 or count % strip:
-            strip -= 16
+            for index in range(4)
+        ]
+
+    def add(target, others, count, keep=None):
+        strip = UNIT
 
         def one(index, carry):
-            at = pl.ds(pl.multiple_of(index * strip, 16), strip)
-            value = stage[pl.ds(pl.multiple_of(first + index * strip, 16), strip)].astype(F32)
-            for ref in [target] + others:
+            at = pl.ds(pl.multiple_of(index * strip, strip), strip)
+            value = target[at].astype(F32)
+            for ref in others:
                 value = value + ref[at].astype(F32)
             if keep is None:
                 target[at] = value.astype(BF16)
@@ -1091,6 +1192,10 @@
         if not (isinstance(step, int) and step == 0):
             out.append((z + step, z + step < depth))
         return out
+
+    def both(step, action):
+        for level, cond in sides(step):
+            when(cond, functools.partial(action, level))
 
     def backwards(body, first, last):
         if depth <= 4:
@@ -1103,164 +1208,168 @@
 
             lax.fori_loop(0, first - last + 1, looped, 0)
 
-    def leaves(step):
-        for level, cond in sides(step):
-            def go(level=level):
-                for other in (1, 0):
-                    ay(level, other).start()
-                    bx(level, other).start()
+    def leaf(step, other, run):
+        def go(level):
+            ay(level, other, run).start()
+            bx(level, other, run).start()
+
+        both(step, go)
+
+    def fetch(step):
+        def go(level):
+            for copy in own_cross(level) + own_line(level):
+                copy.start()
+
+        both(step, go)
+
+    def entry_of(level, way):
+        at_home = (z - 1 == level) if way == 0 else (z + 1 == level)
+        return level if way == 0 else level + (depth - level) * at_home.astype(jnp.int32)
+
+    def beyond(way):
+        return z + 1 < depth if way == 0 else z >= 1
+
+    def zcd(level, way, index, leaf_copy):
+        entry = entry_of(level, way)
+        if leaf_copy:
+            src = rows(level, index // 2, index % 2, start_c, 2 * small)
+        else:
+            src = l_zcd.at[level, index]
+        return remote(
+            src, l_zcd.at[entry, index], zcd_s.at[level, index], zcd_r.at[entry, index],
+            down if way == 0 else up,
+        )
+
+    def zcd_arrived(entry, index):
+        ref = l_zcd.at[entry, index]
+        remote(ref, ref, zcd_s.at[0, index], zcd_r.at[entry, index], up).wait_recv()
+
+    def lines(step):
+        return ((0, z - step, z - step >= 0), (1, z + step, z + step < depth))
+
+    def plane_step(step):
+        for way, level, cond in lines(step):
+            def go(way=way, level=level):
+                @pl.when(beyond(way))
+                def _():
+                    copies = own_plane(level)
+                    for copy in copies:
+                        copy.start()
+                    for index in range(4):
+                        zcd_arrived(level, index)
+                        copies[index].wait()
+                        add(l_zcd.at[level, index], [o_plane.at[level, index]], 2 * small)
+                        zcd(level, way, index, False).start()
+
+                @pl.when(jnp.logical_not(beyond(way)))
+                def _():
+                    for index in range(4):
+                        zcd(level, way, index, True).start()
 
             when(cond, go)
 
-    def zcd(level, way, part):
-        device = down if way == 0 else up
-        beyond = z + 1 < depth if way == 0 else z >= 1
-        at_home = (z - 1 == level) if way == 0 else (z + 1 == level)
-        entry = level if way == 0 else level + (depth - level) * at_home.astype(jnp.int32)
-        dst = l_zcd.at[entry, part]
-        src = rows(level, part // 2, part % 2, start_c, 2 * small)
-        send_sem, recv_sem = zcd_s.at[level, part], zcd_r.at[entry, part]
-        leaf = remote(src, dst, send_sem, recv_sem, device)
-        node = remote(l_zcd.at[level, part], dst, send_sem, recv_sem, device)
-        return beyond, leaf, node, src
-
-    def plane_step(step):
-        for way, level, cond in ((0, z - step, z - step >= 0), (1, z + step, z + step < depth)):
+    def zab(level, way, run):
+        entry = entry_of(level, way)
+        return [
+            remote(
+                landing.at[level, part(run)], l_zab.at[entry, index, part(run)],
+                zab_s.at[level, index, run], zab_r.at[entry, index, run], down if way == 0 else up,
+            )
+            for index, landing in enumerate((l_ax, l_by))
+        ]
+
+    def zab_arrived(entry, index, run):
+        ref = l_zab.at[entry, index, part(run)]
+        remote(ref, ref, zab_s.at[0, index, run], zab_r.at[entry, index, run], up).wait_recv()
+
+    def across(run):
+        def go(level):
+            count = pieces[run][1]
+            copies = own_cross(level)
+            ay(level, 1, run).wait_recv()
+            if run == 0:
+                copies[0].wait()
+            add(l_ay.at[level, 1, part(run)], [o_cross.at[level, 0, part(run)]], count)
+            ax(level, run).start()
+            bx(level, 1, run).wait_recv()
+            if run == 0:
+                copies[1].wait()
+            add(l_bx.at[level, 1, part(run)], [o_cross.at[level, 1, part(run)]], count)
+            by(level, run).start()
+
+        return go
+
+    def line_step(step, run):
+        count = pieces[run][1]
+        for way, level, cond in lines(step):
             def go(way=way, level=level):
-                hops = [zcd(level, way, part) for part in range(4)]
-                beyond = hops[0][0]
-
-                @pl.when(beyond)
-                def _():
-                    copies = fetch([hop[3] for hop in hops])
-                    for part, (_, leaf, node, src) in enumerate(hops):
-                        remote(
-                            l_zcd.at[level, part], l_zcd.at[level, part], zcd_s.at[level, part],
-                            zcd_r.at[level, part], up,
-                        ).wait_recv()
-                        copies[part].wait()
-                        add(l_zcd.at[level, part], part * 2 * small, 2 * small, [])
-                        node.start()
-
-                @pl.when(jnp.logical_not(beyond))
-                def _():
-                    for _, leaf, node, src in hops:
-                        leaf.start()
+                copies = own_line(level)
+                hops = zab(level, way, run)
+                for index, (first_hop, second_hop, first_land, second_land) in enumerate(
+                    ((ay, ax, l_ay, l_ax), (bx, by, l_bx, l_by))
+                ):
+                    first_hop(level, 0, run).wait_recv()
+                    second_hop(level, run).wait_recv()
+                    if run == 0:
+                        copies[index].wait()
+                    target = second_land.at[level, part(run)]
+                    terms = [first_land.at[level, 0, part(run)], o_line.at[level, index, part(run)]]
+
+                    @pl.when(beyond(way))
+                    def _(index=index, target=target, terms=terms):
+                        zab_arrived(level, index, run)
+                        add(target, terms + [l_zab.at[level, index, part(run)]], count)
+
+                    @pl.when(jnp.logical_not(beyond(way)))
+                    def _(target=target, terms=terms):
+                        add(target, terms, count)
+
+                    hops[index].start()
 
             when(cond, go)
 
-    def zab(level, way):
-        device = down if way == 0 else up
-        beyond = z + 1 < depth if way == 0 else z >= 1
-        at_home = (z - 1 == level) if way == 0 else (z + 1 == level)
-        entry = level if way == 0 else level + (depth - level) * at_home.astype(jnp.int32)
-        copies = []
-        for index, landing in enumerate((l_ax, l_by)):
-            copies.append(
-                remote(
-                    landing.at[level], l_zab.at[entry, index], zab_s.at[level, index],
-                    zab_r.at[entry, index], device,
-                )
-            )
-        return beyond, copies
-
-    def zab_arrived(entry, index):
-        remote(
-            l_zab.at[entry, index], l_zab.at[entry, index], zab_s.at[entry, index],
-            zab_r.at[entry, index], up,
-        ).wait_recv()
-
-    def across(level):
-        copies = fetch([rows(level, 1 - x, y, 0, large), rows(level, x, 1 - y, start_b, large)])
-        ay(level, 1).wait_recv()
-        copies[0].wait()
-        add(l_ay.at[level, 1], 0, large, [])
-        ax(level).start()
-        bx(level, 1).wait_recv()
-        copies[1].wait()
-        add(l_bx.at[level, 1], large, large, [])
-        by(level).start()
-
-    def line_step(step):
-        for way, level, cond in ((0, z - step, z - step >= 0), (1, z + step, z + step < depth)):
-            def go(way=way, level=level):
-                copies = fetch([rows(level, x, y, 0, 2 * large)])
-                beyond, hops = zab(level, way)
-                ay(level, 0).wait_recv()
-                ax(level).wait_recv()
-                copies[0].wait()
-
-                @pl.when(beyond)
-                def _():
-                    zab_arrived(level, 0)
-                    add(l_ax.at[level], 0, large, [l_ay.at[level, 0], l_zab.at[level, 0]])
-
-                @pl.when(jnp.logical_not(beyond))
-                def _():
-                    add(l_ax.at[level], 0, large, [l_ay.at[level, 0]])
-
-                hops[0].start()
-                bx(level, 0).wait_recv()
-                by(level).wait_recv()
-
-                @pl.when(beyond)
-                def _():
-                    zab_arrived(level, 1)
-                    add(l_by.at[level], large, large, [l_bx.at[level, 0], l_zab.at[level, 1]])
-
-                @pl.when(jnp.logical_not(beyond))
-                def _():
-                    add(l_by.at[level], large, large, [l_bx.at[level, 0]])
-
-                hops[1].start()
-
-            when(cond, go)
-
-    def both(step, action):
-        for level, cond in sides(step):
-            when(cond, functools.partial(action, level))
+    unrolled = depth <= 4
+    place.enter()
+    for run in runs:
+        leaf(depth - 1, 1, run)
+    if not unrolled:
+        for run in runs:
+            leaf(depth - 1, 0, run)
+    fetch(depth - 1)
 
     def turn(step):
-        leaves(step)
         plane_step(step)
-        both(step, across)
-        line_step(step)
+        for run in runs:
+            if unrolled and step == depth - 1:
+                leaf(step, 0, run)
+            both(step, across(run))
+        for run in runs:
+            leaf(step - 1, 1, run)
+        fetch(step - 1)
+        for run in runs:
+            line_step(step, run)
+            leaf(step - 1, 0, run)
 
     backwards(turn, depth - 1, 1)
-    leaves(0)
-
-    def home(entry, part, cond):
-        def go():
-            remote(
-                l_zcd.at[entry, part], l_zcd.at[entry, part], zcd_s.at[0, part],
-                zcd_r.at[entry, part], up,
-            ).wait_recv()
-
-        when(cond, go)
 
     above, below = z + 1 < depth, z >= 1
-    copies = fetch([rows(z, part // 2, part % 2, start_c, 2 * small) for part in range(4)])
-    for part in range(4):
-        home(z, part, above)
-        home(depth, part, below)
-        copies[part].wait()
-
-        @pl.when(above & below)
-        def _(part=part):
-            add(l_zcd.at[z, part], part * 2 * small, 2 * small, [l_zcd.at[depth, part]])
-
-        @pl.when(above & jnp.logical_not(below))
-        def _(part=part):
-            add(l_zcd.at[z, part], part * 2 * small, 2 * small, [])
-
-        @pl.when(jnp.logical_not(above))
-        def _(part=part):
-            strip = 2 * small
-            value = stage[pl.ds(part * strip, strip)].astype(F32) + l_zcd[depth, part].astype(F32)
-            l_zcd[z, part] = value.astype(BF16)
+    copies = own_plane(z)
+    for copy in copies:
+        copy.start()
+    for index in range(4):
+        pl.when(above)(functools.partial(zcd_arrived, z, index))
+        pl.when(below)(functools.partial(zcd_arrived, depth, index))
+        copies[index].wait()
+        target = o_plane.at[z, index]
+        for cond, entries in (
+            (above & below, (z, depth)), (above & jnp.logical_not(below), (z,)), (jnp.logical_not(above), (depth,))
+        ):
+            @pl.when(cond)
+            def _(entries=entries, target=target, index=index):
+                add(target, [l_zcd.at[entry, index] for entry in entries], 2 * small)
 
     def block_at(xx, yy, first):
-        return l_zcd.at[z, xx * 2 + yy, pl.ds(first, small)]
+        return o_plane.at[z, xx * 2 + yy, pl.ds(first, small)]
 
     plane = [
         remote(block_at(1 - x, 1 - y, 0), l_c.at[1], cd_s.at[0], cd_r.at[0], over_y),
@@ -1272,53 +1381,41 @@
     ]
     for copy in plane[:4]:
         copy.start()
-    both(0, across)
+    for run in runs:
+        both(0, across(run))
     plane[0].wait_recv()
-    l_c[1] = (l_c[1].astype(F32) + l_zcd[z, (1 - x) * 2 + y, pl.ds(0, small)].astype(F32)).astype(BF16)
+    add(l_c.at[1], [block_at(1 - x, y, 0)], small)
     plane[4].start()
     plane[2].wait_recv()
-    l_d[1] = (l_d[1].astype(F32) + l_zcd[z, x * 2 + 1 - y, pl.ds(small, small)].astype(F32)).astype(BF16)
+    add(l_d.at[1], [block_at(x, 1 - y, small)], small)
     plane[5].start()
 
-    copies = fetch([rows(z, x, y, 0, 2 * large)])
-    copies[0].wait()
-    for index, (first_hop, second_hop, first_land, second_land, begin) in enumerate(
-        ((ay, ax, l_ay, l_ax, 0), (bx, by, l_bx, l_by, start_b))
-    ):
-        first_hop(z, 0).wait_recv()
-        second_hop(z).wait_recv()
-        base = [second_land.at[z], first_land.at[z, 0]]
-        target = final.at[pl.ds(begin, large)]
-
-        @pl.when(above)
-        def _(index=index):
-            zab_arrived(z, index)
-
-        @pl.when(below)
-        def _(index=index):
-            zab_arrived(depth, index)
-
-        for cond, more in (
-            (above & below, [z, depth]),
-            (above & jnp.logical_not(below), [z]),
-            (jnp.logical_not(above), [depth]),
+    copies = own_line(z)
+    for run in runs:
+        first, count = pieces[run]
+        for index, (first_hop, second_hop, first_land, second_land) in enumerate(
+            ((ay, ax, l_ay, l_ax), (bx, by, l_bx, l_by))
         ):
-            @pl.when(cond)
-            def _(more=more, base=base, target=target, begin=begin, index=index):
-                add(
-                    base[0], begin, large,
-                    base[1:] + [l_zab.at[entry, index] for entry in more], keep=target,
-                )
+            first_hop(z, 0, run).wait_recv()
+            second_hop(z, run).wait_recv()
+            if run == 0:
+                copies[index].wait()
+            terms = [first_land.at[z, 0, part(run)], o_line.at[z, index, part(run)]]
+            target = final.at[pl.ds(index * large + first, count)]
+            pl.when(above)(functools.partial(zab_arrived, z, index, run))
+            pl.when(below)(functools.partial(zab_arrived, depth, index, run))
+            for cond, entries in (
+                (above & below, (z, depth)), (above & jnp.logical_not(below), (z,)), (jnp.logical_not(above), (depth,))
+            ):
+                @pl.when(cond)
+                def _(entries=entries, terms=terms, target=target, index=index, land=second_land, run=run, count=count):
+                    more = [l_zab.at[entry, index, part(run)] for entry in entries]
+                    add(land.at[z, part(run)], terms + more, count, keep=target)
 
     for copy in (plane[1], plane[3], plane[4], plane[5]):
         copy.wait_recv()
-    here = x * 2 + y
-    final[pl.ds(start_c, small)] = (
-        l_zcd[z, here, pl.ds(0, small)].astype(F32) + l_c[0].astype(F32) + l_c[2].astype(F32)
-    )
-    final[pl.ds(start_d, small)] = (
-        l_zcd[z, here, pl.ds(small, small)].astype(F32) + l_d[0].astype(F32) + l_d[2].astype(F32)
-    )
+    add(block_at(x, y, 0), [l_c.at[0], l_c.at[2]], small, keep=final.at[pl.ds(start_c, small)])
+    add(block_at(x, y, small), [l_d.at[0], l_d.at[2]], small, keep=final.at[pl.ds(start_d, small)])
     own_rows = block // 2
     theirs = final.at[pl.ds(pl.multiple_of((1 - core) * own_rows, 16), own_rows)]
     mine = final.at[pl.ds(pl.multiple_of(core * own_rows, 16), own_rows)]
@@ -1328,24 +1425,25 @@
     local.start()
 
     def drain(step):
-        for level, cond in sides(step):
-            def go(level=level):
+        def go(level):
+            for run in runs:
                 for other in range(2):
-                    ay(level, other).wait_send()
-                    bx(level, other).wait_send()
-                ax(level).wait_send()
-                by(level).wait_send()
-
-            when(cond, go)
+                    ay(level, other, run).wait_send()
+                    bx(level, other, run).wait_send()
+                ax(level, run).wait_send()
+                by(level, run).wait_send()
+
+        both(step, go)
         if not (isinstance(step, int) and step == 0):
-            for way, level, cond in ((0, z - step, z - step >= 0), (1, z + step, z + step < depth)):
-                def go(way=way, level=level):
-                    for part in range(4):
-                        zcd(level, way, part)[2].wait_send()
-                    for copy in zab(level, way)[1]:
-                        copy.wait_send()
-
-                when(cond, go)
+            for way, level, cond in lines(step):
+                def along(way=way, level=level):
+                    for index in range(4):
+                        zcd(level, way, index, False).wait_send()
+                    for run in runs:
+                        for copy in zab(level, way, run):
+                            copy.wait_send()
+
+                when(cond, along)
 
     steps(depth, drain)
     for copy in plane:
@@ -1371,13 +1469,15 @@
         pltpu.VMEM((depth + 1, 4, 2 * small, half), BF16),
         pltpu.VMEM((3, small, half), BF16),
         pltpu.VMEM((3, small, half), BF16),
-        pltpu.VMEM((max(2 * large, 8 * small), half), BF16),
+        pltpu.VMEM((depth, 2, large, half), BF16),
+        pltpu.VMEM((depth, 2, large, half), BF16),
+        pltpu.VMEM((depth, 4, 2 * small, half), BF16),
         pltpu.VMEM((block, half), F32),
         pltpu.VMEM((block // 2, half), F32),
-        dma((4,)), dma((2,)), dma((1,)), dma((1,)),
-        dma((depth, 2)), dma((depth, 2)), dma((depth,)), dma((depth,)),
-        dma((depth, 2)), dma((depth, 2)), dma((depth,)), dma((depth,)),
-        dma((depth + 1, 2)), dma((depth + 1, 2)),
+        dma((depth, 2)), dma((depth, 2)), dma((depth, 4)), dma((2,)), dma((1,)), dma((1,)),
+        dma((depth, 2, 2)), dma((depth, 2, 2)), dma((depth, 2)), dma((depth, 2)),
+        dma((depth, 2, 2)), dma((depth, 2, 2)), dma((depth, 2)), dma((depth, 2)),
+        dma((depth + 1, 2, 2)), dma((depth + 1, 2, 2)),
         dma((depth + 1, 4)), dma((depth + 1, 4)),
         dma((6,)), dma((6,)),
     ]
@@ -1388,7 +1488,7 @@
         out_specs=anywhere,
         scratch_shapes=scratch,
         compiler_params=pltpu.CompilerParams(
-            collective_id=2, has_side_effects=True, vmem_limit_bytes=62 << 20
+            collective_id=2, has_side_effects=True, vmem_limit_bytes=51 << 20
         ),
         name="reduce",
     )(grads)
@@ -1407,8 +1507,28 @@
 
 def update_kernel(
     filled_ref, sums_ref, master_ref, one_ref, two_ref, average_ref,
+    nrm_ref, gain_ref, shift_ref, norm_one_ref, norm_two_ref,
     grad_ref, one_out, two_out, new_ref, average_out, copy_ref,
+    norm_grad_ref, norm_one_out, norm_two_out, norm_new_ref,
 ):
+    @pl.when(pl.program_id(0) == 0)
+    def _():
+        branches = SUBS + SOURCES
+        sums = jnp.concatenate([nrm_ref[0], nrm_ref[1]], axis=1)
+        shifts = sums[branches : branches + SUBS]
+        both = (
+            sums[:branches],
+            jnp.concatenate([shifts] + [shifts[SUBS - 1 :]] * SOURCES, axis=0),
+        )
+        for index, (gradient, params) in enumerate(zip(both, (gain_ref, shift_ref))):
+            moment, second, new = adamw(
+                gradient, params[...], norm_one_ref[:, index], norm_two_ref[:, index], rate_norm, 0.0
+            )
+            norm_grad_ref[:, index] = gradient
+            norm_one_out[:, index] = moment
+            norm_two_out[:, index] = second
+            norm_new_ref[:, index] = new
+
     filled = filled_ref[pl.program_id(0)] > 0
     half = sums_ref.shape[2]
     strip = 32
@@ -1433,24 +1553,30 @@
     lax.fori_loop(0, master_ref.shape[0] // strip, one, 0)
 
 
-def run_update(filled, sums, master, moment_one, moment_two, average):
+def run_update(filled, sums, master, moment_one, moment_two, average, nrm, gains, shifts, norm_one, norm_two):
     rows, width = master.shape
     step = rows // filled.shape[0]
     spec = pl.BlockSpec((step, width), lambda i, t: (i, 0))
+
+    def whole(array):
+        return pl.BlockSpec(array.shape, lambda i, t: (0,) * array.ndim)
+
     grid_spec = pltpu.PrefetchScalarGridSpec(
         num_scalar_prefetch=1,
         grid=(rows // step,),
-        in_specs=[pl.BlockSpec((2, step, sums.shape[2]), lambda i, t: (0, i, 0))] + [spec] * 4,
-        out_specs=[spec] * 6,
+        in_specs=[pl.BlockSpec((2, step, sums.shape[2]), lambda i, t: (0, i, 0))] + [spec] * 4
+        + [whole(array) for array in (nrm, gains, shifts, norm_one, norm_two)],
+        out_specs=[spec] * 6 + [whole(norm_one)] * 4,
     )
     full = jax.ShapeDtypeStruct(master.shape, F32)
     return pl.pallas_call(
         update_kernel,
         grid_spec=grid_spec,
-        out_shape=[full] * 5 + [jax.ShapeDtypeStruct(master.shape, BF16)],
-        compiler_params=pltpu.CompilerParams(vmem_limit_bytes=60 << 20),
+        out_shape=[full] * 5 + [jax.ShapeDtypeStruct(master.shape, BF16)]
+        + [jax.ShapeDtypeStruct(norm_one.shape, F32)] * 4,
+        compiler_params=pltpu.CompilerParams(vmem_limit_bytes=24 << 20),
         name="update",
-    )(filled, sums, master, moment_one, moment_two, average)
+    )(filled, sums, master, moment_one, moment_two, average, nrm, gains, shifts, norm_one, norm_two)
 
 
 def body(
@@ -1482,6 +1608,8 @@
     compact = ((owner // 4) * 2 + owner % 2) * capacity + places % capacity
     parity = (lax.axis_index("wide") // 2) % 2
     handled = jnp.where((owner // 2) % 2 == parity, compact, -1).astype(jnp.int32)
+    kept = 2 * (lax.axis_index("wide") % 2) + lax.axis_index("narrow") // 2
+    handled = jnp.concatenate([handled, kept.astype(jnp.int32)[None]])
     grads = run_grads(wides * narrows * own_rows // 2, handled, act, dcv, res)
     reduced = run_reduce(depth // 2, block, grads)
 
@@ -1489,29 +1617,16 @@
     first = (lax.axis_index("wide") * narrows + lax.axis_index("narrow")) * own_rows
     slot_of_step = (first + step * jnp.arange(own_rows // step, dtype=jnp.int32)) // width
     filled = jnp.any(places[None, :] == slot_of_step[:, None], axis=1).astype(jnp.int32)
-    updated = run_update(filled, reduced, master, moment_one, moment_two, average)
-    sums = sums.transpose(1, 0, 2).reshape(sums.shape[1], -1)
-    branches = SUBS + SOURCES
-    shift_rows = sums[branches : branches + SUBS]
-    norm_grad = jnp.stack(
-        [
-            sums[:branches],
-            jnp.concatenate([shift_rows] + [shift_rows[SUBS - 1 :]] * SOURCES, axis=0),
-        ]
-    )
-    norm_params = jnp.stack([norm_gain, norm_shift])
-    norm_one_new, norm_two_new, norm_new = adamw(
-        norm_grad, norm_params, norm_one, norm_two, rate_norm, 0.0
+    updated = run_update(
+        filled, reduced, master, moment_one, moment_two, average,
+        sums, norm_gain, norm_shift, norm_one.transpose(1, 0, 2), norm_two.transpose(1, 0, 2),
     )
     return (
         block_out,
         input_grad,
         dense_grad,
-        *updated,
-        norm_grad,
-        norm_one_new,
-        norm_two_new,
-        norm_new,
+        *updated[:6],
+        *(values.transpose(1, 0, 2) for values in updated[6:]),
     )
 
 

time: 487 us -> 455 us (0.934)
  Pallas kernels: 478 us -> 446 us
    pallas_call x1, Pallas kernels: 326 us -> 309 us  [run_chain(): pl.pallas_call(functools.partial(chain_kernel, depth, block), out_shape=o...]
    pallas_call x1, Pallas kernels: 111 us -> 104 us  [run_reduce(): pl.pallas_call(functools.partial(reduce_kernel, depth, block), out_shape=...]
    pallas_call x1, Pallas kernels: 14.1 us -> 8.05 us  [run_update(): pl.pallas_call(update_kernel, grid_spec=grid_spec, out_shape=[full] * 5 +...]
where the time goes in v1:
time: 455 us
  Pallas kernels  446 us (98%)
  local copies, waits for them, and re-layouts  4.6 us (1%)
    pallas_call x1, Pallas kernels, run_chain(): pl.pallas_call(functools.partial(chain_kernel, depth, block), out_shape=o...  309 us
    pallas_call x1, Pallas kernels, run_reduce(): pl.pallas_call(functools.partial(reduce_kernel, depth, block), out_shape=...  104 us
    pallas_call x1, Pallas kernels, run_grads(): pl.pallas_call(grad_kernel, grid_spec=grid_spec, out_shape=jax.ShapeDtype...  25 us

profile of v1, /device:TPU:0, one launch (start us, length us, event | category | flops | bytes accessed | tf_op | source)
XLA Modules:
  0.0 454.6 jit_solution(14060782514730246321)
XLA Ops:
  1.4 0.9 select_reduce_fusion
  2.3 0.7 compare_select_fusion.2
  3.0 0.0 copy-start.13
  3.0 0.6 pad_add_fusion.slot_ref
  3.6 0.2 compare_reduce_fusion
  3.8 0.0 copy-done.13
  3.8 309.2 %chain.1 = (bf16[5,2,2,256,512]{4,3,2,1,0:T(8,128)(2,1)}, bf16[5,2,2,288,256]{4,3,2,1,0:T(8,128)(2,1)}, bf16[2,512,256]{2,1,0:T(8,128)(2,1)}, bf16[1,256,512]{2,...) custom-call(s32[89]{0:T(128)} %copy-done.13, s32[1]{0:T(128)S(6)} %copy.29.length_ref, ...), custom_call_target="tpu_custom_call" | custom-call | flops 22817013760 | bytes 16777216 | tf_op jit(solution)/shard_map/chain/pallas_call | solution.py:989
  313.0 25.0 %weight_grads.1.grads = bf16[24576,256]{1,0:T(8,128)(2,1)} custom-call(s32[90]{0:T(128)} %pad_add_fusion.slot_ref, bf16[5,2,2,256,512]{4,3,2,1,0:T(8,128)(2,1)} %get-tuple-element.33.act_ref, bf16[5,2,2,288,256]{4,3,2,1,0:T(8,128)(2,1)} %get-tuple-element.34.dcv_ref, bf16[2,512,256]{2,1,0:T(8,128)(2,1)} %get-tuple-element.35.res_ref), custom_call_target="tpu_custom_call" | custom-call | tf_op jit(solution)/shard_map/weight_grads/pallas_call | solution.py:1083
  338.0 0.0 copy-start.1
  338.0 0.0 copy-start.2
  338.0 0.0 copy-start.3
  338.0 0.0 copy-start.4
  338.0 0.0 copy-start.5
  338.1 0.0 copy-start.6
  338.1 0.0 copy-start.7
  338.1 0.0 copy-start.8
  338.1 0.0 copy-start.9
  338.1 103.8 %reduce.1.sums_ref = f32[2,1536,256]{2,1,0:T(8,128)} custom-call(bf16[24576,256]{1,0:T(8,128)(2,1)} %weight_grads.1.grads), custom_call_target="tpu_custom_call" | custom-call | tf_op jit(solution)/shard_map/reduce/pallas_call | solution.py:1484
  441.9 0.0 copy-done.1
  441.9 0.0 copy-done.2
  441.9 0.0 copy-done.3
  441.9 0.0 copy-done.4
  442.0 0.0 copy-done.5
  442.0 0.0 copy-done.6
  442.0 0.0 copy-done.7
  442.0 0.0 copy-done.8
  442.0 1.9 copy-done
  443.9 8.0 %update.1 = (f32[1536,512]{1,0:T(8,128)}, f32[1536,512]{1,0:T(8,128)}, f32[1536,512]{1,0:T(8,128)}, f32[1536,512]{1,0:T(8,128)}, f32[1536,512]{1,0:T(8,128)}, /*...) custom-call(s32[6]{0:T(128)S(1)} %convert_element_type.3.filled_ref,, ...), custom_call_target="tpu_custom_call" | custom-call | tf_op jit(solution)/shard_map/update/pallas_call | solution.py:1572
  452.0 0.0 copy-done.12
  452.0 0.7 copy.30
  452.7 0.8 copy.31
  453.5 1.1 copy.32
  (9 shorter events, 0.0 us)
Async XLA Ops:
  3.0 0.8 copy-start.13
  338.0 103.9 %copy-start.1 = (f32[1536,512]{1,0:T(8,128)S(1)}, f32[1536,512]{1,0:T(8,128)}, u32[]{:S(2)}) copy-start(f32[1536,512]{1,0:T(8,128)} %master_ref.1) | copy-start | bytes 9437188
  338.0 103.9 %copy-start.2 = (f32[1536,512]{1,0:T(8,128)S(1)}, f32[1536,512]{1,0:T(8,128)}, u32[]{:S(2)}) copy-start(f32[1536,512]{1,0:T(8,128)} %one_ref.1) | copy-start | bytes 9437188
  338.0 103.9 %copy-start.3 = (f32[1536,512]{1,0:T(8,128)S(1)}, f32[1536,512]{1,0:T(8,128)}, u32[]{:S(2)}) copy-start(f32[1536,512]{1,0:T(8,128)} %two_ref.1) | copy-start | bytes 9437188
  338.0 103.9 %copy-start.4 = (f32[1536,512]{1,0:T(8,128)S(1)}, f32[1536,512]{1,0:T(8,128)}, u32[]{:S(2)}) copy-start(f32[1536,512]{1,0:T(8,128)} %average_ref.1) | copy-start | bytes 9437188
  338.0 103.9 %copy-start.5 = (f32[2,11,512]{2,0,1:T(2,128)S(1)}, f32[2,11,512]{2,0,1:T(2,128)}, u32[]{:S(2)}) copy-start(f32[2,11,512]{2,0,1:T(2,128)} %param.24) | copy-start | bytes 135172
  338.1 103.9 %copy-start.6 = (f32[2,11,512]{2,0,1:T(2,128)S(1)}, f32[2,11,512]{2,0,1:T(2,128)}, u32[]{:S(2)}) copy-start(f32[2,11,512]{2,0,1:T(2,128)} %param.25) | copy-start | bytes 135172
  338.1 103.9 %copy-start.7 = (f32[11,512]{1,0:T(8,128)S(1)}, f32[11,512]{1,0:T(8,128)}, u32[]{:S(2)}) copy-start(f32[11,512]{1,0:T(8,128)} %gain_ref.3) | copy-start | bytes 67588
  338.1 103.9 %copy-start.8 = (f32[11,512]{1,0:T(8,128)S(1)}, f32[11,512]{1,0:T(8,128)}, u32[]{:S(2)}) copy-start(f32[11,512]{1,0:T(8,128)} %shift_ref.3) | copy-start | bytes 67588
  338.1 103.9 %copy-start.9 = (f32[2,16,256]{2,1,0:T(8,128)S(1)}, f32[2,16,256]{2,1,0:T(8,128)}, u32[]{:S(2)}) copy-start(f32[2,16,256]{2,1,0:T(8,128)} %get-tuple-element.36.nrm_ref) | copy-start | bytes 98308
  442.0 1.9 copy-start
  443.9 8.1 %copy-start.12 = (bf16[1,256,512]{2,1,0:T(8,128)(2,1)S(1)}, bf16[1,256,512]{2,1,0:T(8,128)(2,1)}, u32[]{:S(2)}) copy-start(bf16[1,256,512]{2,1,0:T(8,128)(2,1)} %get-tuple-element.62) | copy-start | bytes 786436
  443.9 8.8 %copy-start.11 = (f32[1,256,512]{2,1,0:T(8,128)S(1)}, f32[1,256,512]{2,1,0:T(8,128)}, u32[]{:S(2)}) copy-start(f32[1,256,512]{2,1,0:T(8,128)} %get-tuple-element.63) | copy-start | bytes 1572868
  443.9 9.6 %copy-start.10 = (f32[1,256,1536]{2,1,0:T(8,128)S(1)}, f32[1,256,1536]{2,1,0:T(8,128)}, u32[]{:S(2)}) copy-start(f32[1,256,1536]{2,1,0:T(8,128)} %get-tuple-element.64) | copy-start | bytes 4718596

commit v2 on v1

--- a/solution.py
+++ b/solution.py
@@ -89,30 +89,14 @@
     def down(self):
         return self.at(self.z - 1, self.x, self.y, self.core)
 
-    def peer(self, offset):
-        other = lax.rem(self.me + offset, self.groups)
-        return (other // 2, lax.rem(other, 2) * 2 + self.core)
-
-    def enter(self):
-        barrier = pltpu.get_barrier_semaphore()
-        pl.semaphore_signal(barrier, inc=1, device_id=self.partner(), device_id_type=MESH)
-
-        def greet(offset, carry):
-            pl.semaphore_signal(barrier, inc=1, device_id=self.peer(offset), device_id_type=MESH)
-            return carry
-
-        lax.fori_loop(1, self.groups, greet, 0)
-        pl.semaphore_wait(barrier, self.groups)
-
-
-class QuadPlace(Place):
-    def __init__(self, depth):
-        super().__init__(depth)
-        self.parity = lax.rem(self.z, 2)
-        self.z = self.z // 2
-
-    def at(self, z, x, y, core):
-        return ((2 * z + self.parity) * 2 + x, y * 2 + core)
+    def far(self, turn):
+        z = lax.rem(self.z + 1 + turn // 4, self.depth)
+        return self.at(z, lax.rem(turn // 2, 2), lax.rem(turn, 2), self.core)
+
+    def near(self):
+        return (
+            self.over_x(), self.over_y(), self.at(self.z, 1 - self.x, 1 - self.y, self.core)
+        )
 
     def enter(self):
         barrier = pltpu.get_barrier_semaphore()
@@ -127,6 +111,16 @@
         pl.when(below)(functools.partial(greet, self.down()))
         met = 3 + above.astype(jnp.int32) + below.astype(jnp.int32)
         pl.semaphore_wait(barrier, met)
+
+
+class QuadPlace(Place):
+    def __init__(self, depth):
+        super().__init__(depth)
+        self.parity = lax.rem(self.z, 2)
+        self.z = self.z // 2
+
+    def at(self, z, x, y, core):
+        return ((2 * z + self.parity) * 2 + x, y * 2 + core)
 
 
 def remote(src, dst, send_sem, recv_sem, device):
@@ -167,12 +161,24 @@
         lax.fori_loop(max(first, 1), depth, looped, 0)
 
 
+def shares(rows, number):
+    units = rows // UNIT
+    out = []
+    first = 0
+    for index in range(number):
+        count = units // number + (1 if index < units % number else 0)
+        if count:
+            out.append((first * UNIT, count * UNIT))
+        first += count
+    return out
+
+
 def tree_sems(depth):
     dma = pltpu.SemaphoreType.DMA
     return [
-        dma((depth, 2)), dma((depth,)), dma((depth, 2, 4)), dma((depth, 4)),
-        dma((depth,)), dma((depth,)), dma((depth, 2)), dma((depth, 2)),
-        dma((depth,)), dma((depth,)), dma((depth, 2)), dma((depth, 2)),
+        dma((depth, 2, 2)), dma((depth, 2)), dma((depth, 2, 4)), dma((depth, 4)),
+        dma((depth, 2)), dma((depth, 2)), dma((depth, 2, 2)), dma((depth, 2, 2)),
+        dma((depth, 2)), dma((depth, 2)), dma((depth, 2, 2)), dma((depth, 2, 2)),
         dma((6,)), dma((6,)),
     ]
 
@@ -181,6 +187,8 @@
     depth, z, x, y = place.depth, place.z, place.x, place.y
     large, small = cut(block, 9)
     (zab_s, zab_r, zcd_s, zcd_r, ax_s, ax_r, ay_s, ay_r, by_s, by_r, bx_s, bx_r, cd_s, cd_r) = sems
+    pieces = shares(large, 2)
+    runs = range(len(pieces))
 
     def rows(zz, xx, yy, first, count):
         begin = ((zz * 2 + xx) * 2 + yy) * (block // UNIT) + first // UNIT
@@ -190,7 +198,7 @@
         ref = rows(zz, xx, yy, first, count)
         return remote(ref, ref, send_sem, recv_sem, device)
 
-    start_b, start_c, start_d = large, 2 * large, 2 * large + small
+    start_c, start_d = 2 * large, 2 * large + small
     over_x, over_y, up, down = place.over_x(), place.over_y(), place.up(), place.down()
 
     def sides(step):
@@ -199,45 +207,51 @@
             out.append((z + step, z + step < depth))
         return out
 
-    def z_moves(step, kind):
+    def both(step, action):
+        for level, cond in sides(step):
+            when(cond, functools.partial(action, level))
+
+    def z_moves(step, run):
         out = []
         low, high = z - step, z + step
         for level, cond, device, way in (
             (low, (low >= 0) & (z + 1 < depth), up, 0),
             (high, (high < depth) & (z >= 1), down, 1),
         ):
-            if kind == "ab":
-                out.append(
-                    (cond, move(level, x, y, 0, 2 * large, zab_s.at[level, way], zab_r.at[level], device))
+            if run is not None:
+                first, count = pieces[run]
+                copy = move(
+                    level, x, y, 2 * first, 2 * count, zab_s.at[level, way, run], zab_r.at[level, run], device
                 )
-            else:
-                for xx in range(2):
-                    for yy in range(2):
-                        out.append(
-                            (
-                                cond,
-                                move(
-                                    level, xx, yy, start_c, 2 * small,
-                                    zcd_s.at[level, way, xx * 2 + yy],
-                                    zcd_r.at[level, xx * 2 + yy], device,
-                                ),
-                            )
-                        )
+                out.append((cond, copy))
+                continue
+            for index in range(4):
+                copy = move(
+                    level, index // 2, index % 2, start_c, 2 * small, zcd_s.at[level, way, index],
+                    zcd_r.at[level, index], device,
+                )
+                out.append((cond, copy))
         return out
 
-    def ax(level):
-        return move(level, x, y, 0, large, ax_s.at[level], ax_r.at[level], over_x)
-
-    def by(level):
-        return move(level, x, y, start_b, large, by_s.at[level], by_r.at[level], over_y)
-
-    def ay(level, other):
+    def ax(level, run):
+        first, count = pieces[run]
+        return move(level, x, y, 2 * first, count, ax_s.at[level, run], ax_r.at[level, run], over_x)
+
+    def by(level, run):
+        first, count = pieces[run]
+        return move(level, x, y, 2 * first + count, count, by_s.at[level, run], by_r.at[level, run], over_y)
+
+    def ay(level, run, other):
+        first, count = pieces[run]
         xx = 1 - x if other else x
-        return move(level, xx, y, 0, large, ay_s.at[level, other], ay_r.at[level, other], over_y)
-
-    def bx(level, other):
+        return move(level, xx, y, 2 * first, count, ay_s.at[level, run, other], ay_r.at[level, run, other], over_y)
+
+    def bx(level, run, other):
+        first, count = pieces[run]
         yy = 1 - y if other else y
-        return move(level, x, yy, start_b, large, bx_s.at[level, other], bx_r.at[level, other], over_x)
+        return move(
+            level, x, yy, 2 * first + count, count, bx_s.at[level, run, other], bx_r.at[level, run, other], over_x
+        )
 
     plane = [
         move(z, x, y, start_c, small, cd_s.at[0], cd_r.at[0], over_x),
@@ -248,22 +262,29 @@
         move(z, x, 1 - y, start_d, small, cd_s.at[5], cd_r.at[5], over_x),
     ]
 
-    def run(step):
-        if isinstance(step, int) and step == 0:
+    def run_step(step):
+        home = isinstance(step, int) and step == 0
+        if home:
             plane[0].start()
             plane[1].start()
-        else:
-            for level, cond in sides(step):
-                when(cond, move(level, x, y, 0, 2 * large, zab_s.at[level, 0], zab_r.at[level], up).wait_recv)
-        for cond, copy in z_moves(step, "ab"):
-            when(cond, copy.start)
-        for level, cond in sides(step):
-            def begin(level=level):
-                ax(level).start()
-                by(level).start()
-
-            when(cond, begin)
-        if isinstance(step, int) and step == 0:
+        for run in runs:
+            first, count = pieces[run]
+            if not home:
+                both(
+                    step,
+                    lambda level, run=run, first=first, count=count: move(
+                        level, x, y, 2 * first, 2 * count, zab_s.at[level, 0, run], zab_r.at[level, run], up
+                    ).wait_recv(),
+                )
+            for cond, copy in z_moves(step, run):
+                when(cond, copy.start)
+
+            def begin(level, run=run):
+                ax(level, run).start()
+                by(level, run).start()
+
+            both(step, begin)
+        if home:
             first_idle()
             plane[2].start()
             plane[4].start()
@@ -273,48 +294,47 @@
             plane[5].start()
             for copy in plane[2:]:
                 copy.wait_recv()
-            for cond, copy in z_moves(0, "cd"):
+            for cond, copy in z_moves(step, None):
                 when(cond, copy.start)
-        for level, cond in sides(step):
-            def across(level=level):
-                ay(level, 0).start()
-                bx(level, 0).start()
-                ax(level).wait_recv()
-                ay(level, 1).start()
-                by(level).wait_recv()
-                bx(level, 1).start()
-
-            when(cond, across)
-        if isinstance(step, int) and step == 0:
+        for run in runs:
+            def across(level, run=run):
+                ay(level, run, 0).start()
+                bx(level, run, 0).start()
+                ax(level, run).wait_recv()
+                ay(level, run, 1).start()
+                by(level, run).wait_recv()
+                bx(level, run, 1).start()
+
+            both(step, across)
+        if not home:
+            def arrived(level):
+                for index in range(4):
+                    move(
+                        level, x, y, start_c, 2 * small, zcd_s.at[level, 0, index],
+                        zcd_r.at[level, index], up,
+                    ).wait_recv()
+
+            both(step, arrived)
+            for cond, copy in z_moves(step, None):
+                when(cond, copy.start)
+        if home:
             second_idle()
-        if not (isinstance(step, int) and step == 0):
-            for level, cond in sides(step):
-                def arrived(level=level):
-                    for part in range(4):
-                        move(
-                            level, x, y, start_c, 2 * small, zcd_s.at[level, 0, part],
-                            zcd_r.at[level, part], up,
-                        ).wait_recv()
-
-                when(cond, arrived)
-            for cond, copy in z_moves(step, "cd"):
-                when(cond, copy.start)
-
-    steps(depth, run)
+
+    steps(depth, run_step)
 
     def drain(step):
-        for level, cond in sides(step):
-            def finish(level=level):
+        def finish(level):
+            for run in runs:
                 for other in range(2):
-                    ay(level, other).wait_recv()
-                    bx(level, other).wait_recv()
-                    ay(level, other).wait_send()
-                    bx(level, other).wait_send()
-                ax(level).wait_send()
-                by(level).wait_send()
-
-            when(cond, finish)
-        for kind in ("ab", "cd"):
+                    ay(level, run, other).wait_recv()
+                    bx(level, run, other).wait_recv()
+                    ay(level, run, other).wait_send()
+                    bx(level, run, other).wait_send()
+                ax(level, run).wait_send()
+                by(level, run).wait_send()
+
+        both(step, finish)
+        for kind in list(runs) + [None]:
             for cond, copy in z_moves(step, kind):
                 when(cond, copy.wait_send)
 
@@ -352,7 +372,6 @@
     width = 2 * half
     frames = mask.shape[1]
     rows = 2 * frames
-    peers = place.groups - 1
     chunks = dense.shape[0]
     pieces = source_pieces(half)
     inner = pl.ds(EDGE, frames)
@@ -390,18 +409,28 @@
     place.enter()
     base = place.me * (block // UNIT) + core * (own_rows // UNIT)
     units = load_rows // UNIT
-    for copy in mats_in:
-        copy.wait()
+    send_mats = []
     for part in range(loads_of):
         def narrow(unit, carry, part=part):
             at = pl.ds(pl.multiple_of(unit * UNIT, UNIT), UNIT)
             stage[part * units + unit] = side[part * 2 + other, at].astype(BF16)
+            return carry
+
+        def keep_own(unit, carry, part=part):
+            at = pl.ds(pl.multiple_of(unit * UNIT, UNIT), UNIT)
             bank[base + part * units + unit] = side[part * 2 + core, at].astype(BF16)
             return carry
 
-        lax.fori_loop(0, units, narrow, 0)
-    send_mats = remote(stage, bank.at[pl.ds(base, own_rows // UNIT)], swap_s.at[0], swap_r.at[0], partner)
-    send_mats.start()
+        mats_in[2 * part].wait()
+        mats_in[2 * part + 1].wait()
+        lax.fori_loop(0, units, narrow, 0, unroll=2)
+        copy = remote(
+            stage.at[pl.ds(part * units, units)], bank.at[pl.ds(base + part * units, units)],
+            swap_s.at[9 + part], swap_r.at[9 + part], partner,
+        )
+        copy.start()
+        send_mats.append(copy)
+        lax.fori_loop(0, units, keep_own, 0, unroll=2)
     mask[core] = (
         lax.broadcasted_iota(jnp.int32, (frames, 128), 0) < length_ref[0]
     ).astype(F32)
@@ -417,7 +446,8 @@
         return carry
 
     lax.fori_loop(0, SUBS, clear, 0)
-    send_mats.wait()
+    for copy in send_mats:
+        copy.wait()
 
     def prepare():
         for copy in x_in + dense_in + [cot_in]:
@@ -458,7 +488,7 @@
         turned[lax.rem(section, 2)] = jnp.concatenate(
             [act[section, core, u, inner] for u in range(2)], axis=0
         ).T
-        for copy in own_act(section):
+        for copy in own_act(section)[:2]:
             copy.start()
 
     def free_turned(section):
@@ -473,6 +503,7 @@
         for copy in swaps:
             copy.wait()
         turn_act(0)
+        own_act(0)[2].start()
 
     gather_bank(place, bank, block, tree, lambda: swaps.extend(prepare()), arrived)
 
@@ -522,21 +553,24 @@
 
     def share(buffer, index, values):
         buffer[place.me] = values
-
-        def go(offset, carry):
-            remote(
-                buffer.at[place.me], buffer.at[place.me], ex_s.at[index], ex_r.at[index],
-                place.peer(offset),
-            ).start()
+        mine = buffer.at[place.me]
+
+        def go(turn, carry):
+            remote(mine, mine, ex_s.at[index, 1], ex_r.at[index, 1], place.far(turn)).start()
             return carry
 
-        lax.fori_loop(1, place.groups, go, 0, unroll=place.groups <= 16)
-
-    def shared(buffer, index):
-        everyone = buffer.at[pl.ds(0, peers)]
-        copy = remote(everyone, everyone, ex_s.at[index], ex_r.at[index], place.peer(1))
-        copy.wait_recv()
-        copy.wait_send()
+        lax.fori_loop(0, place.groups - 4, go, 0, unroll=place.groups <= 16)
+        for device in place.near():
+            remote(mine, mine, ex_s.at[index, 0], ex_r.at[index, 0], device).start()
+
+    def shared(buffer, index, between=lambda: None):
+        for kind, number in ((0, 3), (1, place.groups - 4)):
+            some = buffer.at[pl.ds(0, number)]
+            copy = remote(some, some, ex_s.at[index, kind], ex_r.at[index, kind], place.over_x())
+            copy.wait_recv()
+            copy.wait_send()
+            if kind == 0:
+                between()
         return buffer[...]
 
     def total_of(values):
@@ -580,26 +614,27 @@
         return keep[row, pl.ds(index, 1)]
 
     count = counted()
-    totals, squares = [], []
-    for index in range(SOURCES):
-        value = None
-        if index < SOURCES - 1:
-            for chunk, lane, lanes in pieces[index]:
-                left = dense[chunk].reshape(rows, half)[:, lane : lane + lanes]
-                right = weight(SUBS * K + chunk // 2, (chunk % 2) * half + lane, lanes)
-                term = jnp.dot(left, right, preferred_element_type=F32)
-                value = term if value is None else value + term
-        else:
-            for h in range(2):
-                left = jnp.concatenate([act[0, h, u, inner] for u in range(2)], axis=0)
-                term = jnp.dot(left, weight(SUBS * K + 3, h * half, half), preferred_element_type=F32)
-                value = term if value is None else value + term
-        side[index] = value
-        total, square = moments(lambda at, index=index: side[index, at], count)
-        totals.append(total)
-        squares.append(square)
-    fill = jnp.zeros((3, half), F32)
-    share(ex_side, 0, jnp.concatenate([count] + totals + squares + [fill], axis=0))
+    def side_branches():
+        totals, squares = [], []
+        for index in range(SOURCES):
+            value = None
+            if index < SOURCES - 1:
+                for chunk, lane, lanes in pieces[index]:
+                    left = dense[chunk].reshape(rows, half)[:, lane : lane + lanes]
+                    right = weight(SUBS * K + chunk // 2, (chunk % 2) * half + lane, lanes)
+                    term = jnp.dot(left, right, preferred_element_type=F32)
+                    value = term if value is None else value + term
+            else:
+                for h in range(2):
+                    left = jnp.concatenate([act[0, h, u, inner] for u in range(2)], axis=0)
+                    term = jnp.dot(left, weight(SUBS * K + 3, h * half, half), preferred_element_type=F32)
+                    value = term if value is None else value + term
+            side[index] = value
+            total, square = moments(lambda at, index=index: side[index, at], count)
+            totals.append(total)
+            squares.append(square)
+        fill = jnp.zeros((3, half), F32)
+        share(ex_side, 0, jnp.concatenate([count] + totals + squares + [fill], axis=0))
 
     def convolve(section, h, first):
         value = None
@@ -634,6 +669,25 @@
         buffer = ex_sub.at[lax.rem(section, 2)]
         share(buffer, 1 + section, jnp.concatenate([count, total, square, jnp.zeros_like(count)], axis=0))
 
+        def pre_side():
+            parts = shared(ex_side, 0)
+            for index in range(SOURCES):
+                mean, inverse, _ = merge(
+                    parts[:, 0], parts[:, 1 + index], parts[:, 1 + SOURCES + index]
+                )
+                save(SUBS + index, mean, inverse)
+            scales = [kept(2, SUBS + index) for index in range(SOURCES)]
+            offset = sum(kept(3, SUBS + index) for index in range(SOURCES))
+
+            def add(at, carry):
+                before = offset
+                for index in range(SOURCES):
+                    before = before + side[index, at] * scales[index]
+                pre4[at] = before
+                return carry
+
+            strips(rows, add)
+
         def background():
             own_act(section - 1)[2].wait_recv()
             pass_act(section - 1).start()
@@ -645,9 +699,14 @@
 
         if isinstance(section, int):
             background()
+            parts = shared(buffer, 1 + section, own_act(section)[2].start)
         else:
+            pl.when(section == 0)(side_branches)
             pl.when(section > 0)(background)
-        parts = shared(buffer, 1 + section)
+            pl.when(section == 1)(pre_side)
+            parts = shared(
+                buffer, 1 + section, lambda: pl.when(section > 0)(own_act(section)[2].start)
+            )
         mean, inverse, frame_total = merge(parts[:, 0], parts[:, 1], parts[:, 2])
         save(section, mean, inverse)
         scale, offset = kept(2, section), kept(3, section)
@@ -679,27 +738,6 @@
 
     def looped(section, carry):
         forward(section, False)
-
-        @pl.when(section == 0)
-        def _():
-            parts = shared(ex_side, 0)
-            for index in range(SOURCES):
-                mean, inverse, _ = merge(
-                    parts[:, 0], parts[:, 1 + index], parts[:, 1 + SOURCES + index]
-                )
-                save(SUBS + index, mean, inverse)
-            scales = [kept(2, SUBS + index) for index in range(SOURCES)]
-            offset = sum(kept(3, SUBS + index) for index in range(SOURCES))
-
-            def add(at, carry):
-                before = offset
-                for index in range(SOURCES):
-                    before = before + side[index, at] * scales[index]
-                pre4[at] = before
-                return carry
-
-            strips(rows, add)
-
         return carry
 
     lax.fori_loop(0, SUBS - 1, looped, 0)
@@ -739,14 +777,14 @@
         up_copy(section).start()
         upown[...] = back_half(section, core)
 
-    def slopes(section, upstream, before_of, others):
+    def slopes(section, upstream, before_of, others, target):
         sources = [(lambda at: raw[section, at], section)] + others
 
         def one(at, carry):
             before = before_of(at)
             sigmoid = jax.nn.sigmoid(before)
             now = upstream(at) * valid(at) * (sigmoid * (1.0 + before * (1.0 - sigmoid)))
-            slope[at] = now
+            target[at] = now
             out = [carry[0] + fold(now)]
             for (load, index), so_far in zip(sources, carry[1:]):
                 out.append(so_far + fold(now * hat_of(load(at), index)))
@@ -755,23 +793,23 @@
         zero = jnp.zeros((8, half), F32)
         return [total_of(value) for value in strips(rows, one, (zero,) * (1 + len(sources)))]
 
-    def branch(load, index, shift_sum, gain_sum, store):
+    def branch(source, load, index, shift_sum, gain_sum, store):
         scale = kept(2, index)
         shift_mean, gain_mean = shift_sum / frame_total, gain_sum / frame_total
 
         def one(at, carry):
-            value = slope[at] - shift_mean - hat_of(load(at), index) * gain_mean
+            value = source[at] - shift_mean - hat_of(load(at), index) * gain_mean
             store(at, (valid(at) * scale * value).astype(BF16))
             return carry
 
         strips(rows, one)
 
-    def conv_branch(section, shift_sum, gain_sum):
+    def conv_branch(source, section, shift_sum, gain_sum):
         def store(at, value):
             first = pl.multiple_of(lax.rem(at.start, frames) + EDGE, EDGE)
             dcv[section, at.start // frames, pl.ds(first, at.size)] = value
 
-        branch(lambda at: raw[section, at], section, shift_sum, gain_sum, store)
+        branch(source, lambda at: raw[section, at], section, shift_sum, gain_sum, store)
         far_dcv(section).start()
         keep_dcv(section).start()
 
@@ -783,23 +821,27 @@
     sums = slopes(
         SUBS - 1, cot_at, lambda at: pre4[at],
         [(lambda at, index=index: side[index, at], SUBS + index) for index in range(SOURCES)],
+        pre4,
     )
     share(ex_last, SUBS + 1, jnp.concatenate(sums, axis=0))
     sums = jnp.sum(shared(ex_last, SUBS + 1), axis=0)
     shift_sum = sums[0:1]
-    conv_branch(SUBS - 1, shift_sum, sums[1:2])
+    conv_branch(pre4, SUBS - 1, shift_sum, sums[1:2])
     nrm[core] = jnp.zeros_like(nrm[0])
     nrm[core, pl.ds(SUBS - 1, 1 + SOURCES)] = sums[1:]
     nrm[core, pl.ds(SUBS + SOURCES + SUBS - 1, 1)] = shift_sum
     backward(SUBS - 1)
-    for index in range(SOURCES):
-        def store(at, value, index=index):
-            dsd[index, at] = value
-
-        branch(
-            lambda at, index=index: side[index, at], SUBS + index, shift_sum,
-            sums[2 + index : 3 + index], store,
-        )
+
+    def side_grads():
+        for index in range(SOURCES):
+            def store(at, value, index=index):
+                dsd[index, at] = value
+
+            branch(
+                pre4, lambda at, index=index: side[index, at], SUBS + index, shift_sum,
+                sums[2 + index : 3 + index], store,
+            )
+
     theirs = pl.multiple_of(other * frames, frames)
     ours = pl.multiple_of(core * frames, frames)
     dg_copy = remote(
@@ -852,16 +894,17 @@
         copy.wait()
         slot = lax.rem(section + 1, 2)
         scale, offset = kept(2, section), kept(3, section)
-        sums = slopes(
+        sums_now = slopes(
             section, lambda at: upown[at] + uprecv[slot, at],
-            lambda at: raw[section, at] * scale + offset, [],
+            lambda at: raw[section, at] * scale + offset, [], slope,
         )
         zero = jnp.zeros((2, half), F32)
         buffer = ex_sub.at[lax.rem(section, 2)]
-        share(buffer, SUBS + 2 + section, jnp.concatenate(sums + [zero], axis=0))
+        share(buffer, SUBS + 2 + section, jnp.concatenate(sums_now + [zero], axis=0))
 
         @pl.when(section == SUBS - 2)
         def _():
+            side_grads()
             residual_grads()
             res_over(0).start()
             dense_grads()
@@ -882,11 +925,11 @@
             res_over(1).wait_recv()
             res_y[...] = (res_y[...].astype(F32) + res_x[place.y].astype(F32)).astype(BF16)
 
-        sums = jnp.sum(shared(buffer, SUBS + 2 + section), axis=0)
+        sums_now = jnp.sum(shared(buffer, SUBS + 2 + section), axis=0)
         pl.when(section == SUBS - 4)(lambda: res_over(2).start())
-        conv_branch(section, sums[0:1], sums[1:2])
-        nrm[core, pl.ds(section, 1)] = sums[1:2]
-        nrm[core, pl.ds(SUBS + SOURCES + section, 1)] = sums[0:1]
+        conv_branch(slope, section, sums_now[0:1], sums_now[1:2])
+        nrm[core, pl.ds(section, 1)] = sums_now[1:2]
+        nrm[core, pl.ds(SUBS + SOURCES + section, 1)] = sums_now[0:1]
 
         @pl.when(section > 0)
         def _():
@@ -977,10 +1020,10 @@
         pltpu.VMEM((groups, 8, half), F32),
         pltpu.VMEM((2, groups, 4, half), F32),
         dma((9 + chunks,)),
-        dma((9,)), dma((9,)),
+        dma((12,)), dma((12,)),
         dma((SUBS,)), dma((SUBS,)),
         dma((2,)), dma((2,)),
-        dma((2 * SUBS + 1,)), dma((2 * SUBS + 1,)),
+        dma((2 * SUBS + 1, 2)), dma((2 * SUBS + 1, 2)),
         dma((10 + chunks,)),
         dma((2 * SUBS + 3,)), dma((2 * SUBS + 3,)),
         dma((2 * SUBS,)), dma((2 * SUBS,)),
@@ -1087,18 +1130,6 @@
         compiler_params=pltpu.CompilerParams(vmem_limit_bytes=60 << 20),
         name="weight_grads",
     )(places, act, dcv, res)
-
-
-def shares(rows, number):
-    units = rows // UNIT
-    out = []
-    first = 0
-    for index in range(number):
-        count = units // number + (1 if index < units % number else 0)
-        if count:
-            out.append((first * UNIT, count * UNIT))
-        first += count
-    return out
 
 
 def reduce_kernel(

time: 455 us -> 445 us (0.978)
  Pallas kernels: 446 us -> 437 us
    pallas_call x1, Pallas kernels: 309 us -> 300 us  [run_chain(): pl.pallas_call(functools.partial(chain_kernel, depth, block), out_shape=o...]
where the time goes in v2:
time: 445 us
  Pallas kernels  437 us (98%)
  local copies, waits for them, and re-layouts  4.6 us (1%)
    pallas_call x1, Pallas kernels, run_chain(): pl.pallas_call(functools.partial(chain_kernel, depth, block), out_shape=o...  300 us
    pallas_call x1, Pallas kernels, run_reduce(): pl.pallas_call(functools.partial(reduce_kernel, depth, block), out_shape=...  103 us
    pallas_call x1, Pallas kernels, run_grads(): pl.pallas_call(grad_kernel, grid_spec=grid_spec, out_shape=jax.ShapeDtype...  25.4 us

profile of v2, /device:TPU:0, one launch (start us, length us, event | category | flops | bytes accessed | tf_op | source)
XLA Modules:
  0.0 445.4 jit_solution(5631656138080278186)
XLA Ops:
  1.4 0.9 select_reduce_fusion
  2.3 0.7 compare_select_fusion.2
  3.0 0.0 copy-start.13
  3.0 0.6 pad_add_fusion.slot_ref
  3.6 0.2 compare_reduce_fusion
  3.8 0.0 copy-done.13
  3.8 300.1 %chain.1 = (bf16[5,2,2,256,512]{4,3,2,1,0:T(8,128)(2,1)}, bf16[5,2,2,288,256]{4,3,2,1,0:T(8,128)(2,1)}, bf16[2,512,256]{2,1,0:T(8,128)(2,1)}, bf16[1,256,512]{2,...) custom-call(s32[89]{0:T(128)} %copy-done.13, s32[1]{0:T(128)S(6)} %copy.29.length_ref, ...), custom_call_target="tpu_custom_call" | custom-call | flops 22817013760 | bytes 16777216 | tf_op jit(solution)/shard_map/chain/pallas_call | solution.py:1032
  303.9 25.4 %weight_grads.1.grads = bf16[24576,256]{1,0:T(8,128)(2,1)} custom-call(s32[90]{0:T(128)} %pad_add_fusion.slot_ref, bf16[5,2,2,256,512]{4,3,2,1,0:T(8,128)(2,1)} %get-tuple-element.33.act_ref, bf16[5,2,2,288,256]{4,3,2,1,0:T(8,128)(2,1)} %get-tuple-element.34.dcv_ref, bf16[2,512,256]{2,1,0:T(8,128)(2,1)} %get-tuple-element.35.res_ref), custom_call_target="tpu_custom_call" | custom-call | tf_op jit(solution)/shard_map/weight_grads/pallas_call | solution.py:1126
  329.3 0.0 copy-start.1
  329.3 0.0 copy-start.2
  329.3 0.0 copy-start.3
  329.3 0.0 copy-start.4
  329.3 0.0 copy-start.5
  329.3 0.0 copy-start.6
  329.4 0.0 copy-start.7
  329.4 0.0 copy-start.8
  329.4 103.3 %reduce.1.sums_ref = f32[2,1536,256]{2,1,0:T(8,128)} custom-call(bf16[24576,256]{1,0:T(8,128)(2,1)} %weight_grads.1.grads), custom_call_target="tpu_custom_call" | custom-call | tf_op jit(solution)/shard_map/reduce/pallas_call | solution.py:1515
  432.7 0.0 copy-done.1
  432.7 0.0 copy-done.2
  432.7 0.0 copy-done.3
  432.7 0.0 copy-done.4
  432.7 0.0 copy-done.5
  432.7 0.0 copy-done.6
  432.7 0.0 copy-done.7
  432.7 0.0 copy-done.8
  432.8 0.0 copy-done.9
  432.8 0.0 copy-start
  432.8 1.9 copy-done
  434.7 8.0 %update.1 = (f32[1536,512]{1,0:T(8,128)}, f32[1536,512]{1,0:T(8,128)}, f32[1536,512]{1,0:T(8,128)}, f32[1536,512]{1,0:T(8,128)}, f32[1536,512]{1,0:T(8,128)}, /*...) custom-call(s32[6]{0:T(128)S(1)} %convert_element_type.3.filled_ref,, ...), custom_call_target="tpu_custom_call" | custom-call | tf_op jit(solution)/shard_map/update/pallas_call | solution.py:1603
  442.7 0.7 copy.30
  443.4 0.8 copy.31
  444.2 1.1 copy.32
  (9 shorter events, 0.0 us)
Async XLA Ops:
  3.0 0.8 copy-start.13
  329.3 103.4 %copy-start.1 = (f32[1536,512]{1,0:T(8,128)S(1)}, f32[1536,512]{1,0:T(8,128)}, u32[]{:S(2)}) copy-start(f32[1536,512]{1,0:T(8,128)} %master_ref.1) | copy-start | bytes 9437188
  329.3 103.4 %copy-start.2 = (f32[1536,512]{1,0:T(8,128)S(1)}, f32[1536,512]{1,0:T(8,128)}, u32[]{:S(2)}) copy-start(f32[1536,512]{1,0:T(8,128)} %one_ref.1) | copy-start | bytes 9437188
  329.3 103.4 %copy-start.3 = (f32[1536,512]{1,0:T(8,128)S(1)}, f32[1536,512]{1,0:T(8,128)}, u32[]{:S(2)}) copy-start(f32[1536,512]{1,0:T(8,128)} %two_ref.1) | copy-start | bytes 9437188
  329.3 103.4 %copy-start.4 = (f32[1536,512]{1,0:T(8,128)S(1)}, f32[1536,512]{1,0:T(8,128)}, u32[]{:S(2)}) copy-start(f32[1536,512]{1,0:T(8,128)} %average_ref.1) | copy-start | bytes 9437188
  329.3 103.4 %copy-start.5 = (f32[2,11,512]{2,0,1:T(2,128)S(1)}, f32[2,11,512]{2,0,1:T(2,128)}, u32[]{:S(2)}) copy-start(f32[2,11,512]{2,0,1:T(2,128)} %param.24) | copy-start | bytes 135172
  329.3 103.4 %copy-start.6 = (f32[2,11,512]{2,0,1:T(2,128)S(1)}, f32[2,11,512]{2,0,1:T(2,128)}, u32[]{:S(2)}) copy-start(f32[2,11,512]{2,0,1:T(2,128)} %param.25) | copy-start | bytes 135172
  329.4 103.4 %copy-start.7 = (f32[11,512]{1,0:T(8,128)S(1)}, f32[11,512]{1,0:T(8,128)}, u32[]{:S(2)}) copy-start(f32[11,512]{1,0:T(8,128)} %gain_ref.3) | copy-start | bytes 67588
  329.4 103.4 %copy-start.8 = (f32[11,512]{1,0:T(8,128)S(1)}, f32[11,512]{1,0:T(8,128)}, u32[]{:S(2)}) copy-start(f32[11,512]{1,0:T(8,128)} %shift_ref.3) | copy-start | bytes 67588
  329.4 103.4 %copy-start.9 = (f32[2,16,256]{2,1,0:T(8,128)S(1)}, f32[2,16,256]{2,1,0:T(8,128)}, u32[]{:S(2)}) copy-start(f32[2,16,256]{2,1,0:T(8,128)} %get-tuple-element.36.nrm_ref) | copy-start | bytes 98308
  432.8 1.9 copy-start
  434.7 8.1 %copy-start.12 = (bf16[1,256,512]{2,1,0:T(8,128)(2,1)S(1)}, bf16[1,256,512]{2,1,0:T(8,128)(2,1)}, u32[]{:S(2)}) copy-start(bf16[1,256,512]{2,1,0:T(8,128)(2,1)} %get-tuple-element.62) | copy-start | bytes 786436
  434.7 8.8 %copy-start.11 = (f32[1,256,512]{2,1,0:T(8,128)S(1)}, f32[1,256,512]{2,1,0:T(8,128)}, u32[]{:S(2)}) copy-start(f32[1,256,512]{2,1,0:T(8,128)} %get-tuple-element.63) | copy-start | bytes 1572868
  434.7 9.6 %copy-start.10 = (f32[1,256,1536]{2,1,0:T(8,128)S(1)}, f32[1,256,1536]{2,1,0:T(8,128)}, u32[]{:S(2)}) copy-start(f32[1,256,1536]{2,1,0:T(8,128)} %get-tuple-element.64) | copy-start | bytes 4718596

commit v3 on v2

--- a/solution.py
+++ b/solution.py
@@ -38,7 +38,7 @@
     same_owner = owners[:, None] == owners[None, :]
     earlier = jnp.arange(number)[None, :] < jnp.arange(number)[:, None]
     ranking = jnp.sum(jnp.where(same_owner & earlier, 1, 0), axis=1)
-    return (owners * capacity + ranking).astype(jnp.int32)
+    return (owners * capacity + ranking).astype(jnp.int32), ranking.astype(jnp.int32)
 
 
 def source_pieces(half):
@@ -1519,7 +1519,7 @@
         out_specs=anywhere,
         scratch_shapes=scratch,
         compiler_params=pltpu.CompilerParams(
-            collective_id=2, has_side_effects=True, vmem_limit_bytes=51 << 20
+            collective_id=2, has_side_effects=True, vmem_limit_bytes=48 << 20
         ),
         name="reduce",
     )(grads)
@@ -1631,14 +1631,13 @@
     own_rows = master.shape[0]
     block = 2 * own_rows
     capacity = own_rows * narrows // width
-    places = slot_table(owners, capacity)
+    places, ranking = slot_table(owners, capacity)
     act, dcv, res, block_out, input_grad, dense_grad, sums = run_chain(
         depth, block, places, lengths, master, inputs, dense_inputs, cotangent, norm_gain, norm_shift
     )
-    owner = places // capacity
-    compact = ((owner // 4) * 2 + owner % 2) * capacity + places % capacity
+    compact = ((owners >> 2) * 2 + (owners & 1)) * capacity + ranking
     parity = (lax.axis_index("wide") // 2) % 2
-    handled = jnp.where((owner // 2) % 2 == parity, compact, -1).astype(jnp.int32)
+    handled = jnp.where(((owners >> 1) & 1) == parity, compact, -1).astype(jnp.int32)
     kept = 2 * (lax.axis_index("wide") % 2) + lax.axis_index("narrow") // 2
     handled = jnp.concatenate([handled, kept.astype(jnp.int32)[None]])
     grads = run_grads(wides * narrows * own_rows // 2, handled, act, dcv, res)

time: 445 us -> 443 us (level)
  no operation moved by 1% of the time
where the time goes in v3:
time: 443 us; the launch traced here: 442 us
  Pallas kernels  436 us (98%)
    pallas_call x1, Pallas kernels, run_chain(): pl.pallas_call(functools.partial(chain_kernel, depth, block), out_shape=o...  300 us
    pallas_call x1, Pallas kernels, run_reduce(): pl.pallas_call(functools.partial(reduce_kernel, depth, block), out_shape=...  102 us
    pallas_call x1, Pallas kernels, run_grads(): pl.pallas_call(grad_kernel, grid_spec=grid_spec, out_shape=jax.ShapeDtype...  25.4 us

profile of v3, /device:TPU:0, one launch (start us, length us, event | category | flops | bytes accessed | tf_op | source)
XLA Modules:
  0.0 442.4 jit_solution(4439635952980976539)
XLA Ops:
  1.4 0.9 select_reduce_fusion
  2.3 0.7 compare_select_fusion
  2.9 0.6 pad_add_fusion.slot_ref
  3.5 0.2 compare_reduce_fusion
  3.7 0.0 copy-done.12
  3.7 300.1 %chain.1 = (bf16[5,2,2,256,512]{4,3,2,1,0:T(8,128)(2,1)}, bf16[5,2,2,288,256]{4,3,2,1,0:T(8,128)(2,1)}, bf16[2,512,256]{2,1,0:T(8,128)(2,1)}, bf16[1,256,512]{2,...) custom-call(s32[89]{0:T(128)} %copy-done.12, s32[1]{0:T(128)S(6)} %copy.29.length_ref, ...), custom_call_target="tpu_custom_call" | custom-call | flops 22817013760 | bytes 16777216 | tf_op jit(solution)/shard_map/chain/pallas_call | solution.py:1032
  303.8 25.4 %weight_grads.1.grads = bf16[24576,256]{1,0:T(8,128)(2,1)} custom-call(s32[90]{0:T(128)} %pad_add_fusion.slot_ref, bf16[5,2,2,256,512]{4,3,2,1,0:T(8,128)(2,1)} %get-tuple-element.33.act_ref, bf16[5,2,2,288,256]{4,3,2,1,0:T(8,128)(2,1)} %get-tuple-element.34.dcv_ref, bf16[2,512,256]{2,1,0:T(8,128)(2,1)} %get-tuple-element.35.res_ref), custom_call_target="tpu_custom_call" | custom-call | tf_op jit(solution)/shard_map/weight_grads/pallas_call | solution.py:1126
  329.2 0.0 copy-start
  329.2 0.0 copy-start.1
  329.2 0.0 copy-start.2
  329.2 0.0 copy-start.3
  329.3 0.0 copy-start.4
  329.3 0.0 copy-start.5
  329.3 0.0 copy-start.6
  329.3 0.0 copy-start.7
  329.3 0.0 copy-start.8
  329.3 102.3 %reduce.1.sums_ref = f32[2,1536,256]{2,1,0:T(8,128)S(1)} custom-call(bf16[24576,256]{1,0:T(8,128)(2,1)} %weight_grads.1.grads), custom_call_target="tpu_custom_call" | custom-call | tf_op jit(solution)/shard_map/reduce/pallas_call | solution.py:1515
  431.6 0.0 copy-done
  431.6 0.0 copy-done.1
  431.6 0.0 copy-done.2
  431.6 0.0 copy-done.3
  431.6 0.0 copy-done.4
  431.6 0.0 copy-done.5
  431.7 0.0 copy-done.6
  431.7 0.0 copy-done.7
  431.7 0.0 copy-done.8
  431.7 0.0 copy-start.11
  431.7 8.1 %update.1 = (f32[1536,512]{1,0:T(8,128)}, f32[1536,512]{1,0:T(8,128)}, f32[1536,512]{1,0:T(8,128)}, f32[1536,512]{1,0:T(8,128)}, f32[1536,512]{1,0:T(8,128)}, /*...) custom-call(s32[6]{0:T(128)S(1)} %convert_element_type.3.filled_ref,, ...), custom_call_target="tpu_custom_call" | custom-call | tf_op jit(solution)/shard_map/update/pallas_call | solution.py:1603
  439.8 0.7 copy.30
  440.5 0.8 copy.31
  441.3 0.0 copy-done.9
  441.3 1.1 copy.32
  (7 shorter events, 0.0 us)
Async XLA Ops:
  2.9 0.8 copy-start.12
  329.2 102.4 %copy-start = (f32[1536,512]{1,0:T(8,128)S(1)}, f32[1536,512]{1,0:T(8,128)}, u32[]{:S(2)}) copy-start(f32[1536,512]{1,0:T(8,128)} %master_ref.1) | copy-start | bytes 9437188
  329.2 102.4 %copy-start.1 = (f32[1536,512]{1,0:T(8,128)S(1)}, f32[1536,512]{1,0:T(8,128)}, u32[]{:S(2)}) copy-start(f32[1536,512]{1,0:T(8,128)} %one_ref.1) | copy-start | bytes 9437188
  329.2 102.4 %copy-start.2 = (f32[1536,512]{1,0:T(8,128)S(1)}, f32[1536,512]{1,0:T(8,128)}, u32[]{:S(2)}) copy-start(f32[1536,512]{1,0:T(8,128)} %two_ref.1) | copy-start | bytes 9437188
  329.2 102.4 %copy-start.3 = (f32[1536,512]{1,0:T(8,128)S(1)}, f32[1536,512]{1,0:T(8,128)}, u32[]{:S(2)}) copy-start(f32[1536,512]{1,0:T(8,128)} %average_ref.1) | copy-start | bytes 9437188
  329.3 102.4 %copy-start.4 = (f32[2,11,512]{2,0,1:T(2,128)S(1)}, f32[2,11,512]{2,0,1:T(2,128)}, u32[]{:S(2)}) copy-start(f32[2,11,512]{2,0,1:T(2,128)} %param.24) | copy-start | bytes 135172
  329.3 102.4 %copy-start.5 = (f32[2,11,512]{2,0,1:T(2,128)S(1)}, f32[2,11,512]{2,0,1:T(2,128)}, u32[]{:S(2)}) copy-start(f32[2,11,512]{2,0,1:T(2,128)} %param.25) | copy-start | bytes 135172
  329.3 102.4 %copy-start.6 = (f32[11,512]{1,0:T(8,128)S(1)}, f32[11,512]{1,0:T(8,128)}, u32[]{:S(2)}) copy-start(f32[11,512]{1,0:T(8,128)} %gain_ref.3) | copy-start | bytes 67588
  329.3 102.4 %copy-start.7 = (f32[11,512]{1,0:T(8,128)S(1)}, f32[11,512]{1,0:T(8,128)}, u32[]{:S(2)}) copy-start(f32[11,512]{1,0:T(8,128)} %shift_ref.3) | copy-start | bytes 67588
  329.3 102.4 %copy-start.8 = (f32[2,16,256]{2,1,0:T(8,128)S(1)}, f32[2,16,256]{2,1,0:T(8,128)}, u32[]{:S(2)}) copy-start(f32[2,16,256]{2,1,0:T(8,128)} %get-tuple-element.36.nrm_ref) | copy-start | bytes 98308
  431.7 8.1 %copy-start.11 = (bf16[1,256,512]{2,1,0:T(8,128)(2,1)S(1)}, bf16[1,256,512]{2,1,0:T(8,128)(2,1)}, u32[]{:S(2)}) copy-start(bf16[1,256,512]{2,1,0:T(8,128)(2,1)} %get-tuple-element.62) | copy-start | bytes 786436
  431.7 8.8 %copy-start.10 = (f32[1,256,512]{2,1,0:T(8,128)S(1)}, f32[1,256,512]{2,1,0:T(8,128)}, u32[]{:S(2)}) copy-start(f32[1,256,512]{2,1,0:T(8,128)} %get-tuple-element.63) | copy-start | bytes 1572868
  431.7 9.6 %copy-start.9 = (f32[1,256,1536]{2,1,0:T(8,128)S(1)}, f32[1,256,1536]{2,1,0:T(8,128)}, u32[]{:S(2)}) copy-start(f32[1,256,1536]{2,1,0:T(8,128)} %get-tuple-element.64) | copy-start | bytes 4718596

commit v4 on v3

--- a/solution.py
+++ b/solution.py
@@ -362,7 +362,7 @@
     act_out, dcv_out, res_out, blk_out, ig_out, dg_out, nrm_out,
     bank, act, dense, mask, cot, raw, side, pre4, slope, upown, upsend, uprecv, dcv, dsd, res, res_x, res_y, dgrecv,
     igrecv, stage, turned, nrm, blk, blksend, keep, ex_side, ex_last, ex_sub,
-    load_sem, swap_s, swap_r, act_s, act_r, up_s, up_r, ex_s, ex_r, out_sem, far_s, far_r, near_s, near_r, own_sem,
+    load_sem, swap_s, swap_r, act_s, act_r, up_s, up_r, ex_s, ex_r, out_sem, far_s, far_r, near_s, near_r, own_sem, edge_sem,
     *tree,
 ):
     place = Place(depth)
@@ -446,6 +446,14 @@
         return carry
 
     lax.fori_loop(0, SUBS, clear, 0)
+    edges = [
+        pltpu.make_async_copy(
+            dcv.at[:, :, pl.ds(first, EDGE)], dcv_out.at[:, 1, :, pl.ds(first, EDGE)], edge_sem.at[index]
+        )
+        for index, first in enumerate((0, EDGE + frames))
+    ]
+    for copy in edges:
+        copy.start()
     for copy in send_mats:
         copy.wait()
 
@@ -516,7 +524,7 @@
 
     def far_dcv(section):
         return remote(
-            dcv.at[section], dcv_out.at[section, 1],
+            dcv.at[section, :, inner], dcv_out.at[section, 1, :, inner],
             far_s.at[SUBS + section], far_r.at[SUBS + section], beside,
         )
 
@@ -966,7 +974,7 @@
     res_over(0).wait_send()
     res_over(1).wait_send()
     res_over(2).wait()
-    for copy in outs + dg_puts:
+    for copy in outs + dg_puts + edges:
         copy.wait()
 
 
@@ -1028,6 +1036,7 @@
         dma((2 * SUBS + 3,)), dma((2 * SUBS + 3,)),
         dma((2 * SUBS,)), dma((2 * SUBS,)),
         dma((2 * SUBS,)),
+        dma((2,)),
     ] + tree_sems(depth)
     return pl.pallas_call(
         functools.partial(chain_kernel, depth, block),
@@ -1216,7 +1225,7 @@
                 keep[at] = value
             return carry
 
-        lax.fori_loop(0, count // strip, one, 0)
+        lax.fori_loop(0, count // strip, one, 0, unroll=4)
 
     def sides(step):
         out = [(z - step, z - step >= 0)]

time: 443 us -> 441 us (level)
  no operation moved by 1% of the time
where the time goes in v4:
time: 441 us
  Pallas kernels  434 us (98%)
    pallas_call x1, Pallas kernels, run_chain(): pl.pallas_call(functools.partial(chain_kernel, depth, block), out_shape=o...  299 us
    pallas_call x1, Pallas kernels, run_reduce(): pl.pallas_call(functools.partial(reduce_kernel, depth, block), out_shape=...  103 us
    pallas_call x1, Pallas kernels, run_grads(): pl.pallas_call(grad_kernel, grid_spec=grid_spec, out_shape=jax.ShapeDtype...  24.7 us

profile of v4, /device:TPU:0, one launch (start us, length us, event | category | flops | bytes accessed | tf_op | source)
XLA Modules:
  0.0 441.0 jit_solution(6668279607826345634)
XLA Ops:
  1.4 0.9 select_reduce_fusion
  2.3 0.7 compare_select_fusion
  2.9 0.6 pad_add_fusion.slot_ref
  3.5 0.2 compare_reduce_fusion
  3.7 0.0 copy-done.12
  3.7 298.5 %chain.1 = (bf16[5,2,2,256,512]{4,3,2,1,0:T(8,128)(2,1)}, bf16[5,2,2,288,256]{4,3,2,1,0:T(8,128)(2,1)}, bf16[2,512,256]{2,1,0:T(8,128)(2,1)}, bf16[1,256,512]{2,...) custom-call(s32[89]{0:T(128)} %copy-done.12, s32[1]{0:T(128)S(6)} %copy.29.length_ref, ...), custom_call_target="tpu_custom_call" | custom-call | flops 22817013760 | bytes 16777216 | tf_op jit(solution)/shard_map/chain/pallas_call | solution.py:1041
  302.3 24.7 %weight_grads.1.grads = bf16[24576,256]{1,0:T(8,128)(2,1)} custom-call(s32[90]{0:T(128)} %pad_add_fusion.slot_ref, bf16[5,2,2,256,512]{4,3,2,1,0:T(8,128)(2,1)} %get-tuple-element.33.act_ref, bf16[5,2,2,288,256]{4,3,2,1,0:T(8,128)(2,1)} %get-tuple-element.34.dcv_ref, bf16[2,512,256]{2,1,0:T(8,128)(2,1)} %get-tuple-element.35.res_ref), custom_call_target="tpu_custom_call" | custom-call | tf_op jit(solution)/shard_map/weight_grads/pallas_call | solution.py:1135
  326.9 0.0 copy-start
  326.9 0.0 copy-start.1
  327.0 0.0 copy-start.2
  327.0 0.0 copy-start.3
  327.0 0.0 copy-start.4
  327.0 0.0 copy-start.5
  327.0 0.0 copy-start.6
  327.0 0.0 copy-start.7
  327.0 0.0 copy-start.8
  327.0 103.1 %reduce.1.sums_ref = f32[2,1536,256]{2,1,0:T(8,128)S(1)} custom-call(bf16[24576,256]{1,0:T(8,128)(2,1)} %weight_grads.1.grads), custom_call_target="tpu_custom_call" | custom-call | tf_op jit(solution)/shard_map/reduce/pallas_call | solution.py:1524
  430.1 0.0 copy-done
  430.1 0.0 copy-done.1
  430.1 0.0 copy-done.2
  430.1 0.0 copy-done.3
  430.1 0.0 copy-done.4
  430.2 0.0 copy-done.5
  430.2 0.0 copy-done.6
  430.2 0.0 copy-done.7
  430.2 0.0 copy-done.8
  430.2 0.0 copy-start.11
  430.2 8.1 %update.1 = (f32[1536,512]{1,0:T(8,128)}, f32[1536,512]{1,0:T(8,128)}, f32[1536,512]{1,0:T(8,128)}, f32[1536,512]{1,0:T(8,128)}, f32[1536,512]{1,0:T(8,128)}, /*...) custom-call(s32[6]{0:T(128)S(1)} %convert_element_type.3.filled_ref,, ...), custom_call_target="tpu_custom_call" | custom-call | tf_op jit(solution)/shard_map/update/pallas_call | solution.py:1612
  438.3 0.7 copy.30
  439.0 0.8 copy.31
  439.8 0.0 copy-done.9
  439.8 1.1 copy.32
  (7 shorter events, 0.0 us)
Async XLA Ops:
  2.9 0.8 copy-start.12
  326.9 103.2 %copy-start = (f32[1536,512]{1,0:T(8,128)S(1)}, f32[1536,512]{1,0:T(8,128)}, u32[]{:S(2)}) copy-start(f32[1536,512]{1,0:T(8,128)} %master_ref.1) | copy-start | bytes 9437188
  326.9 103.2 %copy-start.1 = (f32[1536,512]{1,0:T(8,128)S(1)}, f32[1536,512]{1,0:T(8,128)}, u32[]{:S(2)}) copy-start(f32[1536,512]{1,0:T(8,128)} %one_ref.1) | copy-start | bytes 9437188
  327.0 103.2 %copy-start.2 = (f32[1536,512]{1,0:T(8,128)S(1)}, f32[1536,512]{1,0:T(8,128)}, u32[]{:S(2)}) copy-start(f32[1536,512]{1,0:T(8,128)} %two_ref.1) | copy-start | bytes 9437188
  327.0 103.2 %copy-start.3 = (f32[1536,512]{1,0:T(8,128)S(1)}, f32[1536,512]{1,0:T(8,128)}, u32[]{:S(2)}) copy-start(f32[1536,512]{1,0:T(8,128)} %average_ref.1) | copy-start | bytes 9437188
  327.0 103.2 %copy-start.4 = (f32[2,11,512]{2,0,1:T(2,128)S(1)}, f32[2,11,512]{2,0,1:T(2,128)}, u32[]{:S(2)}) copy-start(f32[2,11,512]{2,0,1:T(2,128)} %param.24) | copy-start | bytes 135172
  327.0 103.2 %copy-start.5 = (f32[2,11,512]{2,0,1:T(2,128)S(1)}, f32[2,11,512]{2,0,1:T(2,128)}, u32[]{:S(2)}) copy-start(f32[2,11,512]{2,0,1:T(2,128)} %param.25) | copy-start | bytes 135172
  327.0 103.2 %copy-start.6 = (f32[11,512]{1,0:T(8,128)S(1)}, f32[11,512]{1,0:T(8,128)}, u32[]{:S(2)}) copy-start(f32[11,512]{1,0:T(8,128)} %gain_ref.3) | copy-start | bytes 67588
  327.0 103.2 %copy-start.7 = (f32[11,512]{1,0:T(8,128)S(1)}, f32[11,512]{1,0:T(8,128)}, u32[]{:S(2)}) copy-start(f32[11,512]{1,0:T(8,128)} %shift_ref.3) | copy-start | bytes 67588
  327.0 103.2 %copy-start.8 = (f32[2,16,256]{2,1,0:T(8,128)S(1)}, f32[2,16,256]{2,1,0:T(8,128)}, u32[]{:S(2)}) copy-start(f32[2,16,256]{2,1,0:T(8,128)} %get-tuple-element.36.nrm_ref) | copy-start | bytes 98308
  430.2 8.1 %copy-start.11 = (bf16[1,256,512]{2,1,0:T(8,128)(2,1)S(1)}, bf16[1,256,512]{2,1,0:T(8,128)(2,1)}, u32[]{:S(2)}) copy-start(bf16[1,256,512]{2,1,0:T(8,128)(2,1)} %get-tuple-element.62) | copy-start | bytes 786436
  430.2 8.8 %copy-start.10 = (f32[1,256,512]{2,1,0:T(8,128)S(1)}, f32[1,256,512]{2,1,0:T(8,128)}, u32[]{:S(2)}) copy-start(f32[1,256,512]{2,1,0:T(8,128)} %get-tuple-element.63) | copy-start | bytes 1572868
  430.2 9.6 %copy-start.9 = (f32[1,256,1536]{2,1,0:T(8,128)S(1)}, f32[1,256,1536]{2,1,0:T(8,128)}, u32[]{:S(2)}) copy-start(f32[1,256,1536]{2,1,0:T(8,128)} %get-tuple-element.64) | copy-start | bytes 4718596

commit v5 on v4

--- a/solution.py
+++ b/solution.py
@@ -572,14 +572,18 @@
             remote(mine, mine, ex_s.at[index, 0], ex_r.at[index, 0], device).start()
 
     def shared(buffer, index, between=lambda: None):
+        sent = []
         for kind, number in ((0, 3), (1, place.groups - 4)):
             some = buffer.at[pl.ds(0, number)]
             copy = remote(some, some, ex_s.at[index, kind], ex_r.at[index, kind], place.over_x())
             copy.wait_recv()
-            copy.wait_send()
+            sent.append(copy)
             if kind == 0:
                 between()
-        return buffer[...]
+        values = buffer[...]
+        for copy in sent:
+            copy.wait_send()
+        return values
 
     def total_of(values):
         return jnp.sum(values, axis=0, keepdims=True)
@@ -1387,8 +1391,9 @@
             leaf(step - 1, 1, run)
         fetch(step - 1)
         for run in runs:
+            leaf(step - 1, 0, run)
+        for run in runs:
             line_step(step, run)
-            leaf(step - 1, 0, run)
 
     backwards(turn, depth - 1, 1)
 

time: 441 us -> 441 us (level)
  no operation moved by 1% of the time
where the time goes in v5:
time: 441 us
  Pallas kernels  434 us (98%)
    pallas_call x1, Pallas kernels, run_chain(): pl.pallas_call(functools.partial(chain_kernel, depth, block), out_shape=o...  299 us
    pallas_call x1, Pallas kernels, run_reduce(): pl.pallas_call(functools.partial(reduce_kernel, depth, block), out_shape=...  103 us
    pallas_call x1, Pallas kernels, run_grads(): pl.pallas_call(grad_kernel, grid_spec=grid_spec, out_shape=jax.ShapeDtype...  24.2 us

profile of v5, /device:TPU:0, one launch (start us, length us, event | category | flops | bytes accessed | tf_op | source)
XLA Modules:
  0.0 440.5 jit_solution(18092704244696597918)
XLA Ops:
  1.4 0.9 select_reduce_fusion
  2.3 0.7 compare_select_fusion
  2.9 0.6 pad_add_fusion.slot_ref
  3.5 0.2 compare_reduce_fusion
  3.7 0.0 copy-done.12
  3.7 298.6 %chain.1 = (bf16[5,2,2,256,512]{4,3,2,1,0:T(8,128)(2,1)}, bf16[5,2,2,288,256]{4,3,2,1,0:T(8,128)(2,1)}, bf16[2,512,256]{2,1,0:T(8,128)(2,1)}, bf16[1,256,512]{2,...) custom-call(s32[89]{0:T(128)} %copy-done.12, s32[1]{0:T(128)S(6)} %copy.29.length_ref, ...), custom_call_target="tpu_custom_call" | custom-call | flops 22817013760 | bytes 16777216 | tf_op jit(solution)/shard_map/chain/pallas_call | solution.py:1045
  302.3 24.2 %weight_grads.1.grads = bf16[24576,256]{1,0:T(8,128)(2,1)} custom-call(s32[90]{0:T(128)} %pad_add_fusion.slot_ref, bf16[5,2,2,256,512]{4,3,2,1,0:T(8,128)(2,1)} %get-tuple-element.33.act_ref, bf16[5,2,2,288,256]{4,3,2,1,0:T(8,128)(2,1)} %get-tuple-element.34.dcv_ref, bf16[2,512,256]{2,1,0:T(8,128)(2,1)} %get-tuple-element.35.res_ref), custom_call_target="tpu_custom_call" | custom-call | tf_op jit(solution)/shard_map/weight_grads/pallas_call | solution.py:1139
  326.5 0.0 copy-start
  326.5 0.0 copy-start.1
  326.5 0.0 copy-start.2
  326.5 0.0 copy-start.3
  326.5 0.0 copy-start.4
  326.5 0.0 copy-start.5
  326.6 0.0 copy-start.6
  326.6 0.0 copy-start.7
  326.6 103.1 %reduce.1.sums_ref = f32[2,1536,256]{2,1,0:T(8,128)S(1)} custom-call(bf16[24576,256]{1,0:T(8,128)(2,1)} %weight_grads.1.grads), custom_call_target="tpu_custom_call" | custom-call | tf_op jit(solution)/shard_map/reduce/pallas_call | solution.py:1529
  429.7 0.0 copy-done
  429.7 0.0 copy-done.1
  429.7 0.0 copy-done.2
  429.7 0.0 copy-done.3
  429.7 0.0 copy-done.4
  429.7 0.0 copy-done.5
  429.7 0.0 copy-done.6
  429.7 0.0 copy-done.7
  429.7 0.0 copy-done.8
  429.7 0.0 copy-start.11
  429.8 0.0 copy-start.10
  429.8 0.0 copy-start.9
  429.8 8.1 %update.1 = (f32[1536,512]{1,0:T(8,128)}, f32[1536,512]{1,0:T(8,128)}, f32[1536,512]{1,0:T(8,128)}, f32[1536,512]{1,0:T(8,128)}, f32[1536,512]{1,0:T(8,128)}, /*...) custom-call(s32[6]{0:T(128)S(1)} %convert_element_type.3.filled_ref,, ...), custom_call_target="tpu_custom_call" | custom-call | tf_op jit(solution)/shard_map/update/pallas_call | solution.py:1617
  437.9 0.7 copy.30
  438.6 0.8 copy.31
  439.4 1.1 copy.32
  (7 shorter events, 0.0 us)
Async XLA Ops:
  2.9 0.8 copy-start.12
  326.5 103.2 %copy-start = (f32[1536,512]{1,0:T(8,128)S(1)}, f32[1536,512]{1,0:T(8,128)}, u32[]{:S(2)}) copy-start(f32[1536,512]{1,0:T(8,128)} %master_ref.1) | copy-start | bytes 9437188
  326.5 103.2 %copy-start.1 = (f32[1536,512]{1,0:T(8,128)S(1)}, f32[1536,512]{1,0:T(8,128)}, u32[]{:S(2)}) copy-start(f32[1536,512]{1,0:T(8,128)} %one_ref.1) | copy-start | bytes 9437188
  326.5 103.2 %copy-start.2 = (f32[1536,512]{1,0:T(8,128)S(1)}, f32[1536,512]{1,0:T(8,128)}, u32[]{:S(2)}) copy-start(f32[1536,512]{1,0:T(8,128)} %two_ref.1) | copy-start | bytes 9437188
  326.5 103.2 %copy-start.3 = (f32[1536,512]{1,0:T(8,128)S(1)}, f32[1536,512]{1,0:T(8,128)}, u32[]{:S(2)}) copy-start(f32[1536,512]{1,0:T(8,128)} %average_ref.1) | copy-start | bytes 9437188
  326.5 103.2 %copy-start.4 = (f32[2,11,512]{2,0,1:T(2,128)S(1)}, f32[2,11,512]{2,0,1:T(2,128)}, u32[]{:S(2)}) copy-start(f32[2,11,512]{2,0,1:T(2,128)} %param.24) | copy-start | bytes 135172
  326.5 103.2 %copy-start.5 = (f32[2,11,512]{2,0,1:T(2,128)S(1)}, f32[2,11,512]{2,0,1:T(2,128)}, u32[]{:S(2)}) copy-start(f32[2,11,512]{2,0,1:T(2,128)} %param.25) | copy-start | bytes 135172
  326.6 103.2 %copy-start.6 = (f32[11,512]{1,0:T(8,128)S(1)}, f32[11,512]{1,0:T(8,128)}, u32[]{:S(2)}) copy-start(f32[11,512]{1,0:T(8,128)} %gain_ref.3) | copy-start | bytes 67588
  326.6 103.2 %copy-start.7 = (f32[11,512]{1,0:T(8,128)S(1)}, f32[11,512]{1,0:T(8,128)}, u32[]{:S(2)}) copy-start(f32[11,512]{1,0:T(8,128)} %shift_ref.3) | copy-start | bytes 67588
  326.6 103.2 %copy-start.8 = (f32[2,16,256]{2,1,0:T(8,128)S(1)}, f32[2,16,256]{2,1,0:T(8,128)}, u32[]{:S(2)}) copy-start(f32[2,16,256]{2,1,0:T(8,128)} %get-tuple-element.36.nrm_ref) | copy-start | bytes 98308
  429.7 8.1 %copy-start.11 = (bf16[1,256,512]{2,1,0:T(8,128)(2,1)S(1)}, bf16[1,256,512]{2,1,0:T(8,128)(2,1)}, u32[]{:S(2)}) copy-start(bf16[1,256,512]{2,1,0:T(8,128)(2,1)} %get-tuple-element.62) | copy-start | bytes 786436
  429.8 8.8 %copy-start.10 = (f32[1,256,512]{2,1,0:T(8,128)S(1)}, f32[1,256,512]{2,1,0:T(8,128)}, u32[]{:S(2)}) copy-start(f32[1,256,512]{2,1,0:T(8,128)} %get-tuple-element.63) | copy-start | bytes 1572868
  429.8 9.6 %copy-start.9 = (f32[1,256,1536]{2,1,0:T(8,128)S(1)}, f32[1,256,1536]{2,1,0:T(8,128)}, u32[]{:S(2)}) copy-start(f32[1,256,1536]{2,1,0:T(8,128)} %get-tuple-element.64) | copy-start | bytes 4718596
